TPU v7x, 256 devices: a whole 4x4x8 slice. The times are simulated.
256 devices in a mesh: row: 16 (over y, x), col: 16 (over z, core).
Axes of the slice: x: 4, y: 4, z: 8, core: 2. Of those that a mesh axis runs over, the one named last changes fastest.
Arguments:
- tensor: float32 [2, 16384, 16384], P(None, 'row', 'col'), may hold values from -6 to 6
- second: float32 [16384, 64], P(('col', 'row')), may hold values from -0.05 to 0.05
- third: float32 [2, 64], replicated, may hold values from 0.5 to 2
Outputs:
- factor: float32 [16384, 64], P(('row', 'col'))
All inputs are finite; a program needn't handle non-finite values.
Results may differ from a plain program's by a relative error of at most 0.00016.
Values sent between devices are 32-bit elements; how exact they have to be, the bound alone decides.
No kernel may reach another device: no remote copies, remote signals or barrier semaphores. Data moves between devices by JAX's collectives and lax.ppermute only.
A program may use at most 64 MiB of HBM per device.

v0:
```python
import jax
import jax.numpy as jnp
from jax import lax
from jax.sharding import PartitionSpec as P


def body(tensor, second, third):
    own_rows = tensor.shape[1]
    block = lax.all_gather(second, "row", axis=0, tiled=True)
    weighted = block[None, :, :] * third[:, None, :]
    local_gram = jnp.dot(
        second.T, second, preferred_element_type=jnp.float32, precision=lax.Precision.HIGHEST
    )
    gram_second = lax.psum(local_gram, ("row", "col"))
    gram_third = jnp.dot(
        third.T, third, preferred_element_type=jnp.float32, precision=lax.Precision.HIGHEST
    )
    gram = gram_second * gram_third
    share = own_rows // lax.axis_size("col")
    summed = lax.psum(
        jnp.einsum(
            "kij,kjr->ir",
            tensor,
            weighted,
            preferred_element_type=jnp.float32,
            precision=lax.Precision.HIGHEST,
        ),
        "col",
    )
    mine = lax.dynamic_slice_in_dim(summed, lax.axis_index("col") * share, share, 0)
    lower = jnp.linalg.cholesky(gram)
    solved = jax.scipy.linalg.cho_solve((lower, True), mine.T)
    return solved.T


def solution(mesh):
    in_specs = (P(None, "row", "col"), P(("col", "row"), None), P())
    out_specs = P(("row", "col"), None)
    return jax.shard_map(body, mesh=mesh, in_specs=in_specs, out_specs=out_specs, check_vma=False)
```

profile of v0, /device:TPU:1, one launch (start us, length us, event | category | flops | bytes accessed | tf_op | source)
XLA Modules:
  0.0 161.9 jit_solution(12667993528695108160)
XLA Ops:
  6.5 0.0 copy-start
  6.5 0.0 copy-start.1
  6.5 0.0 all-reduce.2.cloned.1.call-start
  6.5 20.1 %all_gather.3 = f32[1024,64]{1,0:T(8,128)S(1)} all-gather(f32[64,64]{1,0:T(8,128)} %param.4), channel_id=1, replica_groups=mesh['row'=16,'col'=16] {'row'}, dimensions={0}, use_global_device_ids=true | all-gather | bytes 278528 | tf_op jit(solution)/shard_map/all_gather | solution.py:9
  26.6 11.5 %convolution_bitcast_fusion = f32[1024,64]{0,1:T(8,128)} fusion(f32[2,1024,1024]{2,1,0:T(8,128)} %param.3, f32[2,64]{1,0:T(2,128)} %param.5, f32[1024,64]{1,0:T(8,128)S(1)} %all_gather.3), kind=kOutput, calls=%fused_computation | convolution fusion | flops 1610743808 | bytes 8913408 | tf_op jit(solution)/shard_map/kij,kjr->ir/dot_general | solution.py:21
  38.1 0.0 all-reduce.2.cloned.1.call-update
  38.1 0.0 copy-done
  38.1 0.2 fusion.11
  38.4 83.6 %psum.14 = f32[64,64]{0,1:T(8,128)S(1)} all-reduce(f32[64,64]{0,1:T(8,128)S(1)} %fusion.11), channel_id=1, replica_groups=mesh['row'=16,'col'=16] {'row','col'}, use_global_device_ids=true, to_apply=%region_0.0 | all-reduce | flops 4096 | bytes 32768 | tf_op jit(solution)/shard_map/psum | solution.py:14
  122.0 0.0 copy-done.1
  122.0 0.2 convolution_multiply_fusion
  122.2 0.1 copy.6
  122.3 5.8 %cholesky.16 = f32[64,64]{1,0:T(8,128)S(1)} custom-call(f32[64,64]{1,0:T(8,128)S(1)} %fusion.8), custom_call_target="Cholesky" | custom-call | tf_op jit(solution)/shard_map/jit(cholesky)/cholesky | solution.py:31
  128.2 0.6 compare_reduce_fusion
  128.9 0.7 fusion.3
  129.5 4.9 %custom-call.10 = f32[1,64,64]{1,2,0:T(8,128)S(1)} custom-call(f32[1,64,64]{2,1,0:T(8,128)S(1)} %fusion.3), custom_call_target="InvertDiagBlocksLowerTriangular" | custom-call | tf_op jit(solution)/shard_map/jit(_cho_solve)/triangular_solve | solution.py:32
  134.4 18.7 %all-reduce.2.cloned.1.call-done = f32[1024,64]{0,1:T(8,128)} async-done(((f32[1024,64]{0,1:T(8,128)}), f32[1024,64]{0,1:T(8,128)}) %all-reduce.2.cloned.1.call-update) | async-done | bytes 262160 | tf_op jit(solution)/shard_map/psum | solution.py:20
  153.2 1.0 fusion.6
  154.2 0.9 fusion.4
  (2 shorter events, 0.0 us)
Async XLA Ops:
  6.5 31.6 %copy-start = (f32[64,64]{1,0:T(8,128)S(1)}, f32[64,64]{1,0:T(8,128)}, u32[]{:S(2)}) copy-start(f32[64,64]{1,0:T(8,128)} %param.4) | copy-start | bytes 49156
  6.5 115.5 %copy-start.1 = (f32[2,64]{1,0:T(2,128)S(1)}, f32[2,64]{1,0:T(2,128)}, u32[]{:S(2)}) copy-start(f32[2,64]{1,0:T(2,128)} %param.5) | copy-start | bytes 1540
  6.5 146.6 %all-reduce.2.cloned.1.call-start = ((), (), s32[]{:S(2)}) async-start(), calls=%async_computation | async-start | bytes 524288 | tf_op jit(solution)/shard_map/psum | solution.py:20
Sparse Core Ops, SparseCore 0:
  38.2 114.8 all-reduce.1
where the time goes:
time: 162 us
  blocking collectives  104 us (64%)
  waiting for transfers between devices  18.7 us (12%)
  matrix products  13.8 us (9%)
  between operations  13.5 us (8%)
  other arithmetic  12.1 us (7%)
    psum x1, blocking collectives, body(): gram_second = lax.psum(local_gram, ('row', 'col'))  83.6 us
    all_gather x1, blocking collectives, body(): block = lax.all_gather(second, 'row', axis=0, tiled=True)  20.1 us
    psum x1, waiting for transfers between devices, body(): lax.psum(jnp.einsum('kij,kjr->ir', tensor, weighted, preferred_element_ty...  18.7 us
    dot_general x1, matrix products, body(): jnp.einsum('kij,kjr->ir', tensor, weighted, preferred_element_type=jnp.fl...  11.5 us
    another operation x3, other arithmetic, body(): lower = jnp.linalg.cholesky(gram)  6.52 us
    another operation x2, other arithmetic, body(): solved = jax.scipy.linalg.cho_solve((lower, True), mine.T)  5.57 us
  transfers between devices with their start and end apart: 1, of which 1 were waited for; matrix products, arithmetic and copies ran while one was open for 8% of the time, Pallas kernels for 0%

commit v1 on v0

v1 whole, which is shorter than its diff:
```python
import jax
import jax.numpy as jnp
from jax import lax
from jax.sharding import PartitionSpec as P


def body(tensor, second, third):
    rank = second.shape[1]
    rows = lax.axis_size("row")
    cols = lax.axis_size("col")
    copies = jnp.broadcast_to(second[None], (rows,) + second.shape)
    block = lax.all_to_all(copies, "row", 0, 0).reshape(-1, rank)
    weighted = block[None, :, :] * third[:, None, :]
    local_gram = jnp.dot(
        block.T, block, preferred_element_type=jnp.float32, precision=lax.Precision.HIGHEST
    )
    partial = jnp.einsum(
        "kij,kjr->ir",
        tensor,
        weighted,
        preferred_element_type=jnp.float32,
        precision=lax.Precision.HIGH,
    )
    parts = partial.reshape(cols, -1, rank)
    share = parts.shape[1]
    grams = jnp.broadcast_to(local_gram[None], (cols, rank, rank))
    sent = jnp.concatenate([parts, grams], axis=1)
    got = lax.all_to_all(sent, "col", 0, 0).sum(0)
    mine = got[:share]
    gram_third = jnp.dot(
        third.T, third, preferred_element_type=jnp.float32, precision=lax.Precision.HIGHEST
    )
    gram = got[share:] * gram_third
    lower = jnp.linalg.cholesky(gram)
    return jax.scipy.linalg.cho_solve((lower, True), mine.T).T


def solution(mesh):
    in_specs = (P(None, "row", "col"), P(("col", "row"), None), P())
    out_specs = P(("row", "col"), None)
    return jax.shard_map(body, mesh=mesh, in_specs=in_specs, out_specs=out_specs, check_vma=False)
```

time: 162 us -> 68.7 us (0.42)
  blocking collectives: 104 us -> 42.6 us
  waiting for transfers between devices: 18.7 us -> 0 us
  between operations: 13.5 us -> 0.13 us
  matrix products: 13.8 us -> 9.7 us
  local copies, waits for them, and re-layouts: 0.08 us -> 2.46 us
    psum x1 -> x0, blocking collectives: 83.6 us -> none  [body(): gram_second = lax.psum(local_gram, ('row', 'col'))]
    all_to_all x0 -> x2, blocking collectives: none -> 42.6 us  [the longest x1 27.7 us: body(): got = lax.all_to_all(sent, 'col', 0, 0).sum(0)]
    all_gather x1 -> x0, blocking collectives: 20.1 us -> none  [body(): block = lax.all_gather(second, 'row', axis=0, tiled=True)]
    psum x1 -> x0, waiting for transfers between devices: 18.7 us -> none  [body(): lax.psum(jnp.einsum('kij,kjr->ir', tensor, weighted, preferred_element_ty...]
    dot_general x1, matrix products: 11.5 us -> 7.34 us  [body(): jnp.einsum('kij,kjr->ir', tensor, weighted, preferred_element_type=jnp.fl...]
  transfers between devices with their start and end apart: 1 -> 0, of which waited for: 1 -> 0; matrix products, arithmetic and copies ran while one was open for 8% -> 0% of each run, Pallas kernels for 0% -> 0%
where the time goes in v1:
time: 68.7 us; the launch traced here: 68.5 us
  blocking collectives  42.6 us (62%)
  other arithmetic  13.6 us (20%)
  matrix products  9.7 us (14%)
  local copies, waits for them, and re-layouts  2.46 us (4%)
    all_to_all x1, blocking collectives, body(): got = lax.all_to_all(sent, 'col', 0, 0).sum(0)  27.7 us
    all_to_all x1, blocking collectives, body(): block = lax.all_to_all(copies, 'row', 0, 0).reshape(-1, rank)  14.9 us
    dot_general x1, matrix products, body(): jnp.einsum('kij,kjr->ir', tensor, weighted, preferred_element_type=jnp.fl...  7.34 us
    another operation x3, other arithmetic, body(): lower = jnp.linalg.cholesky(gram)  6.52 us
    another operation x2, other arithmetic, body(): return jax.scipy.linalg.cho_solve((lower, True), mine.T).T  5.55 us

profile of v1, /device:TPU:1, one launch (start us, length us, event | category | flops | bytes accessed | tf_op | source)
XLA Modules:
  0.0 68.5 jit_solution(11206571204178745998)
XLA Ops:
  0.0 0.8 %broadcast_in_dim.5 = f32[16,64,64]{2,1,0:T(8,128)S(1)} broadcast(f32[64,64]{1,0:T(8,128)} %param.4), dimensions={1,2} | broadcast | bytes 278528 | tf_op jit(solution)/shard_map/broadcast_in_dim | solution.py:11
  0.8 0.3 reshape.24
  1.1 14.9 %all_to_all.10 = f32[16,1,4096]{2,1,0:T(1,128)S(1)} all-to-all(f32[16,1,4096]{2,1,0:T(1,128)S(1)} %reshape.24), channel_id=1, replica_groups=mesh['row'=16,'col'=16] {'row'}, dimensions={0} | all-to-all | bytes 524288 | tf_op jit(solution)/shard_map/all_to_all | solution.py:12
  16.1 0.5 broadcast.74
  16.6 1.3 %reduce.6 = f32[16,4096]{1,0:T(8,128)S(1)} reduce(f32[16,1,4096]{2,1,0:T(1,128)S(1)} %all_to_all.10, f32[]{:T(128)} %broadcast.74), dimensions={1}, to_apply=%all_to_all.6.reduce_sub_computation | reduce | bytes 524292 | tf_op jit(solution)/shard_map/all_to_all | solution.py:12
  17.8 0.0 copy-start
  17.9 0.2 reshape.25
  18.1 1.0 %convolution_bitcast_fusion.1 = f32[64,64]{0,1:T(8,128)S(1)} fusion(f32[16,64,64]{2,1,0:T(8,128)S(1)} %reshape.25), kind=kOutput, calls=%fused_computation.2 | convolution fusion | flops 50331648 | bytes 278528 | tf_op jit(solution)/shard_map/dot_general | solution.py:14
  19.1 0.2 copy.9
  19.3 7.3 %convolution_bitcast_fusion = f32[1024,64]{0,1:T(8,128)S(1)} fusion(f32[2,1024,1024]{2,1,0:T(8,128)} %param.3, f32[2,64]{1,0:T(2,128)} %param.5, f32[1024,64]{0,1:T(8,128)S(1)} %copy.9), kind=kOutput, calls=%fused_computation | convolution fusion | flops 805437440 | bytes 8913408 | tf_op jit(solution)/shard_map/kij,kjr->ir/dot_general | solution.py:17
  26.6 0.1 reshape.21
  26.8 0.2 copy.12
  27.0 0.2 pad_maximum_fusion
  27.2 27.7 %all_to_all.11 = f32[16,128,64]{1,2,0:T(8,128)S(1)} all-to-all(f32[16,128,64]{1,2,0:T(8,128)S(1)} %pad_maximum_fusion), channel_id=1, replica_groups=mesh['row'=16,'col'=16] {'col'}, dimensions={0} | all-to-all | bytes 1048576 | tf_op jit(solution)/shard_map/all_to_all | solution.py:28
  54.9 0.0 copy-done
  55.0 0.2 convolution_multiply_fusion
  55.2 0.1 copy.14
  55.3 5.8 %cholesky.16 = f32[64,64]{1,0:T(8,128)S(1)} custom-call(f32[64,64]{1,0:T(8,128)S(1)} %fusion.9), custom_call_target="Cholesky" | custom-call | tf_op jit(solution)/shard_map/jit(cholesky)/cholesky | solution.py:34
  61.2 0.6 compare_reduce_fusion
  61.8 0.7 fusion.3
  62.5 4.9 %custom-call.10 = f32[1,64,64]{1,2,0:T(8,128)S(1)} custom-call(f32[1,64,64]{2,1,0:T(8,128)S(1)} %fusion.3), custom_call_target="InvertDiagBlocksLowerTriangular" | custom-call | tf_op jit(solution)/shard_map/jit(_cho_solve)/triangular_solve | solution.py:35
  67.4 0.3 fusion.4
  67.6 0.9 %fusion.6 = f32[64,64]{1,0:T(8,128)} fusion(f32[64,64]{1,0:T(8,128)S(1)} %fusion.4, f32[1,64,64]{1,2,0:T(8,128)S(1)} %custom-call.10), kind=kOutput, calls=%fused_computation.11 | convolution fusion | flops 3145728 | bytes 49152 | tf_op jit(solution)/shard_map/jit(_cho_solve)/triangular_solve | solution.py:35
  (4 shorter events, 0.1 us)
Async XLA Ops:
  17.8 37.1 %copy-start = (f32[2,64]{1,0:T(2,128)S(1)}, f32[2,64]{1,0:T(2,128)}, u32[]{:S(2)}) copy-start(f32[2,64]{1,0:T(2,128)} %param.5) | copy-start | bytes 1540

commit v2 on v1

v2 whole, which is shorter than its diff:
```python
import jax
import jax.numpy as jnp
from jax import lax
from jax.experimental import pallas as pl
from jax.experimental.pallas import tpu as pltpu
from jax.sharding import PartitionSpec as P

F32 = jnp.float32
BF16 = jnp.bfloat16
RANK = 64
LANES = 128
HALF = 32
STRIP = 8


def vmem():
    return pl.BlockSpec(memory_space=pltpu.VMEM)


def pack_kernel(second_ref, out_ref):
    packed = jnp.concatenate([second_ref[:HALF, :], second_ref[HALF:, :]], axis=1)
    for peer in range(out_ref.shape[0]):
        out_ref[peer] = packed


def swap(x):
    return pltpu.roll(x, RANK, 1)


def product_kernel(tensor_ref, rows_ref, third_ref, out_ref, held, weights, sems):
    slices, own, inner = tensor_ref.shape
    peers = rows_ref.shape[0]
    targets = out_ref.shape[0]
    tile = own // sems.shape[0]
    copies = []
    for t in range(sems.shape[0]):
        part = pl.ds(t * tile, tile)
        copy = pltpu.make_async_copy(tensor_ref.at[:, part], held.at[:, part], sems.at[t])
        copy.start()
        copies.append(copy)

    left = lax.broadcasted_iota(jnp.int32, (HALF, LANES), 1) < RANK
    third = third_ref[...]
    scale = jnp.concatenate([third, third], axis=1)
    for peer in range(peers):
        here = rows_ref[peer]
        there = swap(here)
        for k in range(slices):
            a = here * scale[k : k + 1, :]
            b = there * scale[k : k + 1, :]
            a_hi = a.astype(BF16).astype(F32)
            b_hi = b.astype(BF16).astype(F32)
            first = jnp.where(left, a_hi, b - b_hi)
            other = jnp.where(left, b_hi, a - a_hi)
            base = peer * RANK
            weights[k, base : base + HALF, :] = first.astype(BF16)
            weights[k, base + HALF : base + RANK, :] = other.astype(BF16)

    share = own // targets
    for t in range(sems.shape[0]):
        copies[t].wait()
        total = jnp.zeros((tile, LANES), F32)
        for k in range(slices):
            block = held[k, t * tile : (t + 1) * tile, :]
            hi = block.astype(BF16)
            lo = (block - hi.astype(F32)).astype(BF16)
            w = weights[k]
            total += jnp.dot(hi, w, preferred_element_type=F32)
            total += jnp.dot(lo, w, preferred_element_type=F32)
        total += swap(total)
        for s in range(tile // share):
            upper = total[s * share : s * share + HALF]
            lower = total[s * share + HALF : (s + 1) * share]
            out_ref[t * (tile // share) + s, :HALF, :] = jnp.where(left, upper, lower)

    flat = rows_ref[...].reshape(peers * HALF, LANES)
    both = lax.dot_general(
        flat, flat, (((0,), (0,)), ((), ())),
        precision=lax.Precision.HIGHEST, preferred_element_type=F32,
    )
    outer = lax.dot_general(
        third, third, (((0,), (0,)), ((), ())),
        precision=lax.Precision.HIGHEST, preferred_element_type=F32,
    )
    gram = (both[:RANK, :RANK] + both[RANK:, RANK:]) * outer
    packed = jnp.concatenate([gram[:HALF], gram[HALF:]], axis=1)
    for peer in range(targets):
        out_ref[peer, HALF:, :] = packed


def solve_kernel(got_ref, out_ref):
    total = got_ref[0]
    for peer in range(1, got_ref.shape[0]):
        total = total + got_ref[peer]
    moved = jnp.transpose(jnp.concatenate([total[:HALF]] * 4, axis=0))
    rhs = jnp.concatenate([moved[:RANK, :HALF], moved[RANK:, :HALF]], axis=1)
    gram = jnp.concatenate([total[HALF:, :RANK], total[HALF:, RANK:]], axis=0)
    system = jnp.concatenate([gram, rhs], axis=1)
    strips = RANK // STRIP
    a = [system[STRIP * q : STRIP * (q + 1)] for q in range(strips)]
    row_id = lax.broadcasted_iota(jnp.int32, (STRIP, LANES), 0)
    for p in range(strips):
        cols = [
            [
                jnp.broadcast_to(a[q][:, STRIP * p + m : STRIP * p + m + 1], (STRIP, LANES))
                for m in range(STRIP)
            ]
            for q in range(strips)
        ]
        diag = cols[p]
        piv = a[p]
        for j in range(STRIP):
            inv = 1.0 / jnp.broadcast_to(diag[j][j : j + 1, :], (STRIP, LANES))
            ratio = jnp.where(row_id == j, 1.0 - inv, diag[j] * inv)
            for m in range(j + 1, STRIP):
                diag[m] = diag[m] - ratio * diag[m][j : j + 1, :]
            piv = piv - ratio * piv[j : j + 1, :]
        a[p] = piv
        for q in range(strips):
            if q != p:
                x = a[q]
                for m in range(STRIP):
                    x = x - cols[q][m] * piv[m : m + 1, :]
                a[q] = x
    solved = jnp.concatenate(a, axis=0)
    out_ref[...] = jnp.transpose(jnp.concatenate([solved, solved], axis=0))[RANK:, :RANK]


def body(tensor, second, third):
    rows = lax.axis_size("row")
    cols = lax.axis_size("col")
    slices, own, inner = tensor.shape
    copies = pl.pallas_call(
        pack_kernel,
        out_shape=jax.ShapeDtypeStruct((rows, HALF, LANES), F32),
        in_specs=[vmem()],
        out_specs=vmem(),
    )(second)
    block = lax.all_to_all(copies, "row", 0, 0)
    sent = pl.pallas_call(
        product_kernel,
        out_shape=jax.ShapeDtypeStruct((cols, 2 * HALF, LANES), F32),
        in_specs=[pl.BlockSpec(memory_space=pl.ANY), vmem(), vmem()],
        out_specs=vmem(),
        scratch_shapes=[
            pltpu.VMEM((slices, own, inner), F32),
            pltpu.VMEM((slices, inner, LANES), BF16),
            pltpu.SemaphoreType.DMA((4,)),
        ],
        compiler_params=pltpu.CompilerParams(vmem_limit_bytes=40 << 20),
    )(tensor, block, third)
    got = lax.all_to_all(sent, "col", 0, 0)
    return pl.pallas_call(
        solve_kernel,
        out_shape=jax.ShapeDtypeStruct((RANK, RANK), F32),
        in_specs=[vmem()],
        out_specs=vmem(),
    )(got)


def solution(mesh):
    in_specs = (P(None, "row", "col"), P(("col", "row"), None), P())
    out_specs = P(("row", "col"), None)
    return jax.shard_map(body, mesh=mesh, in_specs=in_specs, out_specs=out_specs, check_vma=False)
```

time: 68.7 us -> 57 us (0.83)
  other arithmetic: 13.6 us -> 0 us
  matrix products: 9.7 us -> 0 us
  Pallas kernels: 0 us -> 9.66 us
  local copies, waits for them, and re-layouts: 2.46 us -> 4.06 us
    another operation x5 -> x0, other arithmetic: 12.1 us -> none  [the longest x3 6.52 us: body(): lower = jnp.linalg.cholesky(gram)]
    pallas_call x0 -> x3, Pallas kernels: none -> 9.66 us  [the longest x1 4.3 us: body(): pl.pallas_call(product_kernel, out_shape=jax.ShapeDtypeStruct((cols, 2 *...]
    dot_general x3 -> x0, matrix products: 8.6 us -> none  [the longest x1 7.34 us: body(): jnp.einsum('kij,kjr->ir', tensor, weighted, preferred_element_type=jnp.fl...]
    unnamed x4, local copies, waits for them, and re-layouts: 0.54 us -> 4.06 us
    all_to_all x1 -> x0, other arithmetic: 1.26 us -> none  [body(): block = lax.all_to_all(copies, 'row', 0, 0).reshape(-1, rank)]
    another operation x2 -> x0, matrix products: 1.1 us -> none  [body(): return jax.scipy.linalg.cho_solve((lower, True), mine.T).T]
    broadcast_in_dim x2 -> x0, local copies, waits for them, and re-layouts: 0.84 us -> none  [the longest x1 0.8 us: body(): copies = jnp.broadcast_to(second[None], (rows,) + second.shape)]
where the time goes in v2:
time: 57 us; the launch traced here: 56.7 us
  blocking collectives  42.9 us (75%)
  Pallas kernels  9.66 us (17%)
  local copies, waits for them, and re-layouts  4.06 us (7%)
    all_to_all x1, blocking collectives, body(): got = lax.all_to_all(sent, 'col', 0, 0)  27.8 us
    all_to_all x1, blocking collectives, body(): block = lax.all_to_all(copies, 'row', 0, 0)  15.1 us
    pallas_call x1, Pallas kernels, body(): pl.pallas_call(product_kernel, out_shape=jax.ShapeDtypeStruct((cols, 2 *...  4.3 us
    unnamed x4, local copies, waits for them, and re-layouts  4.06 us
    pallas_call x1, Pallas kernels, body(): pl.pallas_call(solve_kernel, out_shape=jax.ShapeDtypeStruct((RANK, RANK),...  3.83 us
    pallas_call x1, Pallas kernels, body(): pl.pallas_call(pack_kernel, out_shape=jax.ShapeDtypeStruct((rows, HALF, L...  1.54 us

profile of v2, /device:TPU:1, one launch (start us, length us, event | category | flops | bytes accessed | tf_op | source)
XLA Modules:
  0.0 56.7 jit_solution(14537609838252796628)
XLA Ops:
  0.0 1.5 %shard_map.37 = f32[16,32,128]{2,1,0:T(8,128)} custom-call(f32[64,64]{1,0:T(8,128)} %second_ref.1), custom_call_target="tpu_custom_call" | custom-call | tf_op jit(solution)/shard_map/pallas_call | solution.py:133
  1.5 15.1 %all_to_all.10.rows_ref = f32[16,32,128]{2,1,0:T(8,128)S(1)} all-to-all(f32[16,32,128]{2,1,0:T(8,128)} %shard_map.37), channel_id=1, replica_groups=mesh['row'=16,'col'=16] {'row'}, dimensions={0} | all-to-all | bytes 524288 | tf_op jit(solution)/shard_map/all_to_all | solution.py:139
  16.7 0.0 copy-start
  16.7 3.4 %copy-done = f32[2,1024,1024]{2,1,0:T(8,128)S(1)} copy-done((f32[2,1024,1024]{2,1,0:T(8,128)S(1)}, f32[2,1024,1024]{2,1,0:T(8,128)}, u32[]{:S(2)}) %copy-start) | copy-done | bytes 8388632
  20.0 0.0 copy-start.1
  20.0 0.7 %copy-done.1 = f32[2,64]{1,0:T(2,128)S(1)} copy-done((f32[2,64]{1,0:T(2,128)S(1)}, f32[2,64]{1,0:T(2,128)}, u32[]{:S(2)}) %copy-start.1) | copy-done | bytes 536
  20.7 4.3 %shard_map.38 = f32[16,64,128]{2,1,0:T(8,128)S(1)} custom-call(f32[2,1024,1024]{2,1,0:T(8,128)S(1)} %copy-done, f32[16,32,128]{2,1,0:T(8,128)S(1)} %all_to_all.10.rows_ref, f32[2,64]{1,0:T(2,128)S(1)} %copy-done.1), custom_call_target="tpu_custom_call" | custom-call | tf_op jit(solution)/shard_map/pallas_call | solution.py:140
  25.0 27.8 %all_to_all.11.got_ref = f32[16,64,128]{2,1,0:T(8,128)} all-to-all(f32[16,64,128]{2,1,0:T(8,128)S(1)} %shard_map.38), channel_id=1, replica_groups=mesh['row'=16,'col'=16] {'col'}, dimensions={0} | all-to-all | bytes 1048576 | tf_op jit(solution)/shard_map/all_to_all | solution.py:152
  52.8 3.8 %shard_map.39 = f32[64,64]{1,0:T(8,128)} custom-call(f32[16,64,128]{2,1,0:T(8,128)} %all_to_all.11.got_ref), custom_call_target="tpu_custom_call" | custom-call | tf_op jit(solution)/shard_map/pallas_call | solution.py:153
Async XLA Ops:
  16.7 3.4 %copy-start = (f32[2,1024,1024]{2,1,0:T(8,128)S(1)}, f32[2,1024,1024]{2,1,0:T(8,128)}, u32[]{:S(2)}) copy-start(f32[2,1024,1024]{2,1,0:T(8,128)} %tensor_ref.1) | copy-start | bytes 25165828
  20.0 0.7 %copy-start.1 = (f32[2,64]{1,0:T(2,128)S(1)}, f32[2,64]{1,0:T(2,128)}, u32[]{:S(2)}) copy-start(f32[2,64]{1,0:T(2,128)} %third_ref.1) | copy-start | bytes 1540

commit v3 on v2

v3 whole, which is shorter than its diff:
```python
import jax
import jax.numpy as jnp
from jax import lax
from jax.experimental import pallas as pl
from jax.experimental.pallas import tpu as pltpu
from jax.sharding import PartitionSpec as P

F32 = jnp.float32
BF16 = jnp.bfloat16
RANK = 64
LANES = 128
HALF = 32
STRIP = 8
GROUP = 4


def vmem():
    return pl.BlockSpec(memory_space=pltpu.VMEM)


def limit(mib):
    return pltpu.CompilerParams(vmem_limit_bytes=mib << 20)


def pack_kernel(second_ref, third_ref, out_ref, scale_ref):
    packed = jnp.concatenate([second_ref[:HALF, :], second_ref[HALF:, :]], axis=1)
    for peer in range(out_ref.shape[0]):
        out_ref[peer] = packed
    slices = third_ref.shape[0]
    scale_ref[:slices, :RANK] = third_ref[...]
    scale_ref[:slices, RANK:] = third_ref[...]


def swap(x):
    return pltpu.roll(x, RANK, 1)


def lower_lanes(rows):
    return lax.broadcasted_iota(jnp.int32, (rows, LANES), 1) < RANK


def make_weights(rows_ref, scale_ref, weights):
    left = lower_lanes(HALF)
    for peer in range(rows_ref.shape[0]):
        here = rows_ref[peer]
        there = swap(here)
        for k in range(weights.shape[0]):
            a = here * scale_ref[k : k + 1, :]
            b = there * scale_ref[k : k + 1, :]
            a_hi = a.astype(BF16).astype(F32)
            b_hi = b.astype(BF16).astype(F32)
            first = jnp.where(left, a_hi, b - b_hi)
            other = jnp.where(left, b_hi, a - a_hi)
            base = peer * RANK
            weights[k, base : base + HALF, :] = first.astype(BF16)
            weights[k, base + HALF : base + RANK, :] = other.astype(BF16)


def multiply(held, weights, out_ref, group):
    left = lower_lanes(HALF)
    total = jnp.zeros((GROUP * RANK, LANES), F32)
    for k in range(weights.shape[0]):
        block = held[k, group * GROUP * RANK : (group + 1) * GROUP * RANK, :]
        high = block.astype(BF16)
        low = (block - high.astype(F32)).astype(BF16)
        w = weights[k]
        total += jnp.dot(high, w, preferred_element_type=F32)
        total += jnp.dot(low, w, preferred_element_type=F32)
    total += swap(total)
    for s in range(GROUP):
        upper = total[s * RANK : s * RANK + HALF]
        lower = total[s * RANK + HALF : (s + 1) * RANK]
        out_ref[group * GROUP + s] = jnp.where(left, upper, lower)


def partner_kernel(tensor_ref, rows_ref, scale_ref, out_ref, weights, held, other, sems):
    chips = out_ref.shape[0] - 1
    core = lax.rem(lax.axis_index("col"), 2)
    copies = []
    for turn, (buffer, side) in enumerate(((other, 1 - core), (held, core))):
        for chip in range(chips):
            start = pl.multiple_of(chip * 2 * RANK + side * RANK, RANK)
            copy = pltpu.make_async_copy(
                tensor_ref.at[:, pl.ds(start, RANK)],
                buffer.at[:, pl.ds(chip * RANK, RANK)],
                sems.at[turn * chips + chip],
            )
            copy.start()
            copies.append(copy)
    make_weights(rows_ref, scale_ref, weights)

    flat = rows_ref[...].reshape(-1, LANES)
    both = lax.dot_general(
        flat, flat, (((0,), (0,)), ((), ())),
        precision=lax.Precision.HIGHEST, preferred_element_type=F32,
    )
    third = scale_ref[: weights.shape[0], :]
    outer = lax.dot_general(
        third, third, (((0,), (0,)), ((), ())),
        precision=lax.Precision.HIGHEST, preferred_element_type=F32,
    )
    gram = (both[:RANK, :RANK] + both[RANK:, RANK:]) * outer[:RANK, :RANK]
    out_ref[chips] = jnp.concatenate([gram[:HALF], gram[HALF:]], axis=1)

    for group in range(chips // GROUP):
        for s in range(GROUP):
            copies[group * GROUP + s].wait()
        multiply(other, weights, out_ref, group)
    for chip in range(chips):
        copies[chips + chip].wait()


def own_kernel(held, weights, out_ref):
    for group in range(out_ref.shape[0] // GROUP):
        multiply(held, weights, out_ref, group)


def join_kernel(own_ref, theirs_ref, got_ref, out_ref):
    chips = own_ref.shape[0]
    gram = theirs_ref[chips] + got_ref[chips]
    for chip in range(chips):
        out_ref[chip, :HALF, :] = own_ref[chip] + got_ref[chip]
        out_ref[chip, HALF:, :] = gram


def solve_kernel(got_ref, out_ref):
    total = got_ref[0]
    for peer in range(1, got_ref.shape[0]):
        total = total + got_ref[peer]
    moved = jnp.transpose(jnp.concatenate([total[:HALF]] * 4, axis=0))
    rhs = jnp.concatenate([moved[:RANK, :HALF], moved[RANK:, :HALF]], axis=1)
    gram = jnp.concatenate([total[HALF:, :RANK], total[HALF:, RANK:]], axis=0)
    system = jnp.concatenate([gram, rhs], axis=1)
    strips = RANK // STRIP
    a = [system[STRIP * q : STRIP * (q + 1)] for q in range(strips)]
    row_id = lax.broadcasted_iota(jnp.int32, (STRIP, LANES), 0)
    for p in range(strips):
        cols = [
            [
                jnp.broadcast_to(a[q][:, STRIP * p + m : STRIP * p + m + 1], (STRIP, LANES))
                for m in range(STRIP)
            ]
            for q in range(strips)
        ]
        diag = cols[p]
        piv = a[p]
        for j in range(STRIP):
            inv = 1.0 / jnp.broadcast_to(diag[j][j : j + 1, :], (STRIP, LANES))
            ratio = jnp.where(row_id == j, 1.0 - inv, diag[j] * inv)
            for m in range(j + 1, STRIP):
                diag[m] = diag[m] - ratio * diag[m][j : j + 1, :]
            piv = piv - ratio * piv[j : j + 1, :]
        a[p] = piv
        for q in range(strips):
            if q != p:
                x = a[q]
                for m in range(STRIP):
                    x = x - cols[q][m] * piv[m : m + 1, :]
                a[q] = x
    solved = jnp.concatenate(a, axis=0)
    out_ref[...] = jnp.transpose(jnp.concatenate([solved, solved], axis=0))[RANK:, :RANK]


def shape(*dims, dtype=F32):
    return jax.ShapeDtypeStruct(dims, dtype)


def body(tensor, second, third):
    rows = lax.axis_size("row")
    cols = lax.axis_size("col")
    chips = cols // 2
    slices, own, inner = tensor.shape
    copies, scale = pl.pallas_call(
        pack_kernel,
        out_shape=(shape(rows, HALF, LANES), shape(STRIP, LANES)),
        in_specs=[vmem(), vmem()],
        out_specs=(vmem(), vmem()),
        compiler_params=limit(4),
    )(second, third)
    block = lax.all_to_all(copies, "row", 0, 0)
    theirs, weights, held = pl.pallas_call(
        partner_kernel,
        out_shape=(
            shape(chips + 1, HALF, LANES),
            shape(slices, inner, LANES, dtype=BF16),
            shape(slices, own // 2, inner),
        ),
        in_specs=[pl.BlockSpec(memory_space=pl.ANY), vmem(), vmem()],
        out_specs=(vmem(), vmem(), vmem()),
        scratch_shapes=[
            pltpu.VMEM((slices, own // 2, inner), F32),
            pltpu.SemaphoreType.DMA((cols,)),
        ],
        compiler_params=limit(16),
        cost_estimate=pl.CostEstimate(flops=0, bytes_accessed=8 << 20, transcendentals=0),
    )(pltpu.with_memory_space_constraint(tensor, pltpu.HBM), block, scale)
    got = lax.ppermute(theirs, "col", [(i, i ^ 1) for i in range(cols)])
    mine = pl.pallas_call(
        own_kernel,
        out_shape=shape(chips, HALF, LANES),
        in_specs=[vmem(), vmem()],
        out_specs=vmem(),
        compiler_params=limit(8),
        cost_estimate=pl.CostEstimate(flops=0, bytes_accessed=8 << 20, transcendentals=0),
    )(held, weights)
    sent = pl.pallas_call(
        join_kernel,
        out_shape=shape(chips, 2 * HALF, LANES),
        in_specs=[vmem(), vmem(), vmem()],
        out_specs=vmem(),
        compiler_params=limit(4),
    )(mine, theirs, got)
    sides = [[2 * chip + core for chip in range(chips)] for core in range(2)]
    total = lax.all_to_all(sent, "col", 0, 0, axis_index_groups=sides)
    return pl.pallas_call(
        solve_kernel,
        out_shape=shape(RANK, RANK),
        in_specs=[vmem()],
        out_specs=vmem(),
        compiler_params=limit(4),
    )(total)


def solution(mesh):
    in_specs = (P(None, "row", "col"), P(("col", "row"), None), P())
    out_specs = P(("row", "col"), None)
    return jax.shard_map(body, mesh=mesh, in_specs=in_specs, out_specs=out_specs, check_vma=False)
```

time: 57 us -> 47.5 us (0.83)
  blocking collectives: 42.9 us -> 35.3 us
  local copies, waits for them, and re-layouts: 4.06 us -> 1.44 us
  starting transfers between devices: 0 us -> 2.19 us
  Pallas kernels: 9.66 us -> 8.28 us
    all_to_all x1, blocking collectives: 27.8 us -> 20.3 us  [body(): total = lax.all_to_all(sent, 'col', 0, 0, axis_index_groups=sides)]
    unnamed x4, local copies, waits for them, and re-layouts: 4.06 us -> 1.44 us
    ppermute x0 -> x1, starting transfers between devices: none -> 2.19 us  [body(): got = lax.ppermute(theirs, 'col', [(i, i ^ 1) for i in range(cols)])]
    pallas_call x3 -> x5, Pallas kernels: 9.66 us -> 8.28 us  [the longest x1 4.03 us: body(): pl.pallas_call(partner_kernel, out_shape=(shape(chips + 1, HALF, LANES),...]
  transfers between devices with their start and end apart: 0 -> 1, of which waited for: 0 -> 0; matrix products, arithmetic and copies ran while one was open for 0% -> 0% of each run, Pallas kernels for 0% -> 3%
where the time goes in v3:
time: 47.5 us; the launch traced here: 47.2 us
  blocking collectives  35.3 us (74%)
  Pallas kernels  8.28 us (17%)
  starting transfers between devices  2.19 us (5%)
  local copies, waits for them, and re-layouts  1.44 us (3%)
    all_to_all x1, blocking collectives, body(): total = lax.all_to_all(sent, 'col', 0, 0, axis_index_groups=sides)  20.3 us
    all_to_all x1, blocking collectives, body(): block = lax.all_to_all(copies, 'row', 0, 0)  14.9 us
    pallas_call x1, Pallas kernels, body(): pl.pallas_call(partner_kernel, out_shape=(shape(chips + 1, HALF, LANES),...  4.03 us
    pallas_call x1, Pallas kernels, body(): pl.pallas_call(solve_kernel, out_shape=shape(RANK, RANK), in_specs=[vmem(...  2.78 us
    ppermute x1, starting transfers between devices, body(): got = lax.ppermute(theirs, 'col', [(i, i ^ 1) for i in range(cols)])  2.19 us
    unnamed x4, local copies, waits for them, and re-layouts  1.44 us
    pallas_call x1, Pallas kernels, body(): pl.pallas_call(own_kernel, out_shape=shape(chips, HALF, LANES), in_specs=...  1.37 us
  transfers between devices with their start and end apart: 1, of which 0 were waited for; matrix products, arithmetic and copies ran while one was open for 0% of the time, Pallas kernels for 3%

profile of v3, /device:TPU:1, one launch (start us, length us, event | category | flops | bytes accessed | tf_op | source)
XLA Modules:
  0.0 47.2 jit_solution(5926648383626650547)
XLA Ops:
  0.0 0.0 copy-start
  0.0 0.8 %copy-done = f32[64,64]{1,0:T(8,128)S(1)} copy-done((f32[64,64]{1,0:T(8,128)S(1)}, f32[64,64]{1,0:T(8,128)}, u32[]{:S(2)}) %copy-start) | copy-done | bytes 16408
  0.8 0.0 copy-start.1
  0.8 0.7 %copy-done.1 = f32[2,64]{1,0:T(2,128)S(1)} copy-done((f32[2,64]{1,0:T(2,128)S(1)}, f32[2,64]{1,0:T(2,128)}, u32[]{:S(2)}) %copy-start.1) | copy-done | bytes 536
  1.4 0.1 shard_map.37
  1.5 14.9 %all_to_all.10.rows_ref = f32[16,32,128]{2,1,0:T(8,128)S(1)} all-to-all(f32[16,32,128]{2,1,0:T(8,128)S(1)} %get-tuple-element.10), channel_id=1, replica_groups=mesh['row'=16,'col'=16] {'row'}, dimensions={0} | all-to-all | bytes 524288 | tf_op jit(solution)/shard_map/all_to_all | solution.py:180
  16.5 4.0 %shard_map.38 = (f32[9,32,128]{2,1,0:T(8,128)S(1)}, bf16[2,1024,128]{2,1,0:T(8,128)(2,1)S(1)}, f32[2,512,1024]{2,1,0:T(8,128)S(1)}) custom-call(f32[2,1024,1024]{2,1,0:T(8,128)} %tensor_ref.1, f32[16,32,128]{2,1,0:T(8,128)S(1)} %all_to_all.10.rows_ref, f32[8,128]{1,0:T(8,128)S(1)} %get-tuple-element.11.scale_ref), custom_call_target="tpu_custom_call" | custom-call | bytes 8388608 | tf_op jit(solution)/shard_map/pallas_call | solution.py:181
  20.5 2.2 %collective-permute-start = (f32[9,32,128]{2,1,0:T(8,128)S(1)}, f32[9,32,128]{2,1,0:T(8,128)S(1)}, u32[]{:S(2)}, u32[]{:S(2)}) collective-permute-start(f32[9,32,128]{2,1,0:T(8,128)S(1)} %get-tuple-element.14.theirs_ref), channel_id=1, source_target_pairs={{0,1},{1,0},{2,3},{3,2},{4,5},{5,4},{6,7},{7,6},{8,9},{9,8},{10,11... | collective-permute-start | bytes 442376 | tf_op jit(solution)/shard_map/ppermute | solution.py:197
  22.7 1.4 %shard_map.39.own_ref = f32[8,32,128]{2,1,0:T(8,128)S(1)} custom-call(f32[2,512,1024]{2,1,0:T(8,128)S(1)} %get-tuple-element.12.held, bf16[2,1024,128]{2,1,0:T(8,128)(2,1)S(1)} %get-tuple-element.13.weights), custom_call_target="tpu_custom_call" | custom-call | bytes 8388608 | tf_op jit(solution)/shard_map/pallas_call | solution.py:198
  24.1 0.0 collective-permute-done.got_ref
  24.1 20.3 %all_to_all.11.got_ref = f32[8,64,128]{2,1,0:T(8,128)S(1)} all-to-all(f32[8,64,128]{2,1,0:T(8,128)S(1)} %shard_map.40), channel_id=1, replica_groups={{0,2,4,6,8,10,12,14},{1,3,5,7,9,11,13,15},{16,18,20,22,24,26,28,30},{17..., dimensions={0} | all-to-all | bytes 524288 | tf_op jit(solution)/shard_map/all_to_all | solution.py:214
  44.5 2.8 %shard_map.41 = f32[64,64]{1,0:T(8,128)} custom-call(f32[8,64,128]{2,1,0:T(8,128)S(1)} %all_to_all.11.got_ref), custom_call_target="tpu_custom_call" | custom-call | tf_op jit(solution)/shard_map/pallas_call | solution.py:215
  (1 shorter events, 0.0 us)
Async XLA Ops:
  0.0 0.8 %copy-start = (f32[64,64]{1,0:T(8,128)S(1)}, f32[64,64]{1,0:T(8,128)}, u32[]{:S(2)}) copy-start(f32[64,64]{1,0:T(8,128)} %second_ref.1) | copy-start | bytes 49156
  0.8 0.7 %copy-start.1 = (f32[2,64]{1,0:T(2,128)S(1)}, f32[2,64]{1,0:T(2,128)}, u32[]{:S(2)}) copy-start(f32[2,64]{1,0:T(2,128)} %third_ref.1) | copy-start | bytes 1540
  20.5 3.6 %collective-permute-start = (f32[9,32,128]{2,1,0:T(8,128)S(1)}, f32[9,32,128]{2,1,0:T(8,128)S(1)}, u32[]{:S(2)}, u32[]{:S(2)}) collective-permute-start(f32[9,32,128]{2,1,0:T(8,128)S(1)} %get-tuple-element.14.theirs_ref), channel_id=1, source_target_pairs={{0,1},{1,0},{2,3},{3,2},{4,5},{5,4},{6,7},{7,6},{8,9},{9,8},{10,11... | collective-permute-start | bytes 442376 | tf_op jit(solution)/shard_map/ppermute | solution.py:197

commit v4 on v3

v4 whole, which is shorter than its diff:
```python
import jax
import jax.numpy as jnp
from jax import lax
from jax.experimental import pallas as pl
from jax.experimental.pallas import tpu as pltpu
from jax.sharding import PartitionSpec as P

F32 = jnp.float32
BF16 = jnp.bfloat16
RANK = 64
LANES = 128
HALF = 32
STRIP = 8
GROUP = 4
GRAM_ROWS = 24


def vmem():
    return pl.BlockSpec(memory_space=pltpu.VMEM)


def anywhere():
    return pl.BlockSpec(memory_space=pl.ANY)


def in_hbm(x):
    return pltpu.with_memory_space_constraint(x, pltpu.HBM)


def limit(mib):
    return pltpu.CompilerParams(vmem_limit_bytes=mib << 20)


def shape(*dims, dtype=F32):
    return jax.ShapeDtypeStruct(dims, dtype)


def pack_kernel(second_ref, out_ref):
    packed = jnp.concatenate([second_ref[:HALF, :], second_ref[HALF:, :]], axis=1)
    for peer in range(out_ref.shape[0]):
        out_ref[peer] = packed


def swap(x):
    return pltpu.roll(x, RANK, 1)


def lower_lanes(rows):
    return lax.broadcasted_iota(jnp.int32, (rows, LANES), 1) < RANK


def make_weights(rows_ref, scale, weights):
    left = lower_lanes(HALF)
    for peer in range(rows_ref.shape[0]):
        here = rows_ref[peer]
        there = swap(here)
        for k in range(weights.shape[0]):
            a = here * scale[k : k + 1, :]
            b = there * scale[k : k + 1, :]
            a_hi = a.astype(BF16).astype(F32)
            b_hi = b.astype(BF16).astype(F32)
            first = jnp.where(left, a_hi, b - b_hi)
            other = jnp.where(left, b_hi, a - a_hi)
            base = peer * RANK
            weights[k, base : base + HALF, :] = first.astype(BF16)
            weights[k, base + HALF : base + RANK, :] = other.astype(BF16)


def multiply(tensor_ref, weights, out_ref, first, side):
    left = lower_lanes(HALF)
    total = jnp.zeros((GROUP * RANK, LANES), F32)
    for k in range(weights.shape[0]):
        block = jnp.concatenate(
            [
                tensor_ref[k, pl.ds(pl.multiple_of((2 * chip + side) * RANK, RANK), RANK), :]
                for chip in range(first, first + GROUP)
            ],
            axis=0,
        )
        high = block.astype(BF16)
        low = (block - high.astype(F32)).astype(BF16)
        w = weights[k]
        total += jnp.dot(high, w, preferred_element_type=F32)
        total += jnp.dot(low, w, preferred_element_type=F32)
    total += swap(total)
    for s in range(GROUP):
        upper = total[s * RANK : s * RANK + HALF]
        lower = total[s * RANK + HALF : (s + 1) * RANK]
        out_ref[(first + s) * HALF : (first + s + 1) * HALF, :] = jnp.where(left, upper, lower)


def pack_gram(gram):
    quarter = HALF // 4
    top = jnp.concatenate([gram[: HALF // 2], gram[HALF // 2 : HALF]], axis=1)
    corner = [
        gram[HALF + quarter * b : HALF + quarter * (b + 1), HALF:] for b in range(4)
    ]
    return jnp.concatenate([top, jnp.concatenate(corner, axis=1)], axis=0)


def partner_kernel(tensor_ref, rows_ref, third_ref, out_ref, weights, scale, sem):
    core = lax.rem(lax.axis_index("col"), 2)
    slices = weights.shape[0]
    copy = pltpu.make_async_copy(third_ref, scale.at[:slices, :], sem)
    copy.start()
    flat = rows_ref[...].reshape(-1, LANES)
    both = lax.dot_general(
        flat, flat, (((0,), (0,)), ((), ())),
        precision=lax.Precision.HIGHEST, preferred_element_type=F32,
    )
    copy.wait()
    third = scale[:slices, :]
    outer = lax.dot_general(
        third, third, (((0,), (0,)), ((), ())),
        precision=lax.Precision.HIGHEST, preferred_element_type=F32,
    )
    gram = (both[:RANK, :RANK] + both[RANK:, RANK:]) * outer
    out_ref[2 * GROUP * HALF :, :] = pack_gram(gram)
    make_weights(rows_ref, jnp.concatenate([third, third], axis=1), weights)
    for first in range(0, 2 * GROUP, GROUP):
        multiply(tensor_ref, weights, out_ref, first, 1 - core)


def own_kernel(tensor_ref, weights, out_ref):
    core = lax.rem(lax.axis_index("col"), 2)
    for first in range(0, 2 * GROUP, GROUP):
        multiply(tensor_ref, weights, out_ref, first, core)


def join_kernel(own_ref, theirs_ref, got_ref, out_ref):
    chips = out_ref.shape[0]
    gram = theirs_ref[chips * HALF :, :] + got_ref[chips * HALF :, :]
    for chip in range(chips):
        part = slice(chip * HALF, (chip + 1) * HALF)
        out_ref[chip, :HALF, :] = own_ref[part, :] + got_ref[part, :]
        out_ref[chip, HALF:, :] = gram


def lane(x, c):
    return jnp.broadcast_to(x[:, c : c + 1], (STRIP, LANES))


def pairwise(terms):
    while len(terms) > 1:
        terms = [terms[i] + terms[i + 1] for i in range(0, len(terms), 2)]
    return terms[0]


def eliminate(diag, others, row_id):
    diag = list(diag)
    for j in range(STRIP):
        inv = 1.0 / jnp.broadcast_to(diag[j][j : j + 1, :], (STRIP, LANES))
        ratio = jnp.where(row_id == j, 1.0 - inv, diag[j] * inv)
        for m in range(j + 1, STRIP):
            diag[m] = diag[m] - ratio * diag[m][j : j + 1, :]
        others = [x - ratio * x[j : j + 1, :] for x in others]
    return others


def solve_kernel(got_ref, out_ref):
    total = pairwise([got_ref[peer] for peer in range(got_ref.shape[0])])
    moved = jnp.transpose(jnp.concatenate([total[:HALF]] * 4, axis=0))
    rhs = jnp.concatenate([moved[:RANK, :HALF], moved[RANK:, :HALF]], axis=1)
    top = total[HALF : HALF + HALF // 2]
    corner = total[HALF + HALF // 2 :]
    upper = jnp.concatenate([top[:, :RANK], top[:, RANK:]], axis=0)
    beside = jnp.transpose(upper[:, HALF:])
    below = jnp.concatenate([corner[:, HALF * b : HALF * (b + 1)] for b in range(4)], axis=0)
    lower = jnp.concatenate([beside, below], axis=1)
    system = jnp.concatenate([jnp.concatenate([upper, lower], axis=0), rhs], axis=1)
    strips = RANK // STRIP
    a = [system[STRIP * q : STRIP * (q + 1)] for q in range(strips)]
    row_id = lax.broadcasted_iota(jnp.int32, (STRIP, LANES), 0)
    diag = [lane(a[0], m) for m in range(STRIP)]
    for p in range(strips):
        base = STRIP * p
        cols = [
            [lane(a[q], base + m) for m in range(STRIP)] if q != p else None
            for q in range(strips)
        ]
        ahead = []
        if p + 1 < strips:
            ahead = [lane(a[p], base + STRIP + m) for m in range(STRIP)]
            old = [lane(a[p + 1], base + STRIP + m) for m in range(STRIP)]
        pivot, *ahead = eliminate(diag, [a[p]] + ahead, row_id)
        a[p] = pivot
        if p + 1 < strips:
            diag = [
                old[m]
                - pairwise([cols[p + 1][k] * ahead[m][k : k + 1, :] for k in range(STRIP)])
                for m in range(STRIP)
            ]
        for q in range(strips):
            if q != p:
                a[q] = a[q] - pairwise(
                    [cols[q][m] * pivot[m : m + 1, :] for m in range(STRIP)]
                )
    solved = jnp.concatenate(a, axis=0)
    out_ref[...] = jnp.transpose(jnp.concatenate([solved, solved], axis=0))[RANK:, :RANK]


def body(tensor, second, third):
    rows = lax.axis_size("row")
    cols = lax.axis_size("col")
    chips = cols // 2
    slices, own, inner = tensor.shape
    pairs = [(i, i ^ 1) for i in range(cols)]
    second, tensor = lax.optimization_barrier((lax.ppermute(second, "col", pairs), tensor))
    tensor = lax.ppermute(tensor, "col", pairs)
    copies = pl.pallas_call(
        pack_kernel,
        out_shape=shape(rows, HALF, LANES),
        in_specs=[vmem()],
        out_specs=vmem(),
        compiler_params=limit(4),
    )(second)
    block = lax.all_to_all(copies, "row", 0, 0)
    theirs, weights = pl.pallas_call(
        partner_kernel,
        out_shape=(
            shape(chips * HALF + GRAM_ROWS, LANES),
            shape(slices, inner, LANES, dtype=BF16),
        ),
        in_specs=[vmem(), vmem(), anywhere()],
        out_specs=(vmem(), vmem()),
        scratch_shapes=[pltpu.VMEM((STRIP, RANK), F32), pltpu.SemaphoreType.DMA],
        compiler_params=limit(12),
        cost_estimate=pl.CostEstimate(flops=0, bytes_accessed=4 << 20, transcendentals=0),
    )(tensor, block, in_hbm(third))
    got = lax.ppermute(theirs, "col", pairs)
    mine = pl.pallas_call(
        own_kernel,
        out_shape=shape(chips * HALF, LANES),
        in_specs=[vmem(), vmem()],
        out_specs=vmem(),
        compiler_params=limit(12),
        cost_estimate=pl.CostEstimate(flops=0, bytes_accessed=4 << 20, transcendentals=0),
    )(tensor, weights)
    sent = pl.pallas_call(
        join_kernel,
        out_shape=shape(chips, HALF + GRAM_ROWS, LANES),
        in_specs=[vmem(), vmem(), vmem()],
        out_specs=vmem(),
        compiler_params=limit(4),
    )(mine, theirs, got)
    sides = [[2 * chip + core for chip in range(chips)] for core in range(2)]
    total = lax.all_to_all(sent, "col", 0, 0, axis_index_groups=sides)
    return pl.pallas_call(
        solve_kernel,
        out_shape=shape(RANK, RANK),
        in_specs=[vmem()],
        out_specs=vmem(),
        compiler_params=limit(4),
    )(total)


def solution(mesh):
    in_specs = (P(None, "row", "col"), P(("col", "row"), None), P())
    out_specs = P(("row", "col"), None)
    return jax.shard_map(body, mesh=mesh, in_specs=in_specs, out_specs=out_specs, check_vma=False)
```

time: 47.5 us -> 45.4 us (0.956)
  starting transfers between devices: 2.19 us -> 4.96 us
  blocking collectives: 35.3 us -> 32.8 us
  Pallas kernels: 8.28 us -> 6.4 us
  local copies, waits for them, and re-layouts: 1.44 us -> 0 us
  waiting for transfers between devices: 0.01 us -> 1.08 us
    ppermute x1 -> x3, starting transfers between devices: 2.19 us -> 4.96 us  [the longest x1 3.24 us: body(): lax.ppermute(second, 'col', pairs)]
    all_to_all x1, blocking collectives: 14.9 us -> 13.2 us  [body(): block = lax.all_to_all(copies, 'row', 0, 0)]
    pallas_call x4, Pallas kernels: 5.5 us -> 3.92 us  [the longest x1 2.43 us: body(): pl.pallas_call(partner_kernel, out_shape=(shape(chips * HALF + GRAM_ROWS,...]
    unnamed x4 -> x0, local copies, waits for them, and re-layouts: 1.44 us -> none
    ppermute x1 -> x3, waiting for transfers between devices: 0.01 us -> 1.08 us  [the longest x1 1.07 us: body(): lax.ppermute(second, 'col', pairs)]
    all_to_all x1, blocking collectives: 20.3 us -> 19.6 us  [body(): total = lax.all_to_all(sent, 'col', 0, 0, axis_index_groups=sides)]
  transfers between devices with their start and end apart: 1 -> 3, of which waited for: 0 -> 1; matrix products, arithmetic and copies ran while one was open for 0% -> 0% of each run, Pallas kernels for 3% -> 3%
where the time goes in v4:
time: 45.4 us; the launch traced here: 45.3 us
  blocking collectives  32.8 us (72%)
  Pallas kernels  6.4 us (14%)
  starting transfers between devices  4.96 us (11%)
  waiting for transfers between devices  1.08 us (2%)
    all_to_all x1, blocking collectives, body(): total = lax.all_to_all(sent, 'col', 0, 0, axis_index_groups=sides)  19.6 us
    all_to_all x1, blocking collectives, body(): block = lax.all_to_all(copies, 'row', 0, 0)  13.2 us
    ppermute x1, starting transfers between devices, body(): lax.ppermute(second, 'col', pairs)  3.24 us
    pallas_call x1, Pallas kernels, body(): pl.pallas_call(solve_kernel, out_shape=shape(RANK, RANK), in_specs=[vmem(...  2.48 us
    pallas_call x1, Pallas kernels, body(): pl.pallas_call(partner_kernel, out_shape=(shape(chips * HALF + GRAM_ROWS,...  2.43 us
    pallas_call x1, Pallas kernels, body(): pl.pallas_call(own_kernel, out_shape=shape(chips * HALF, LANES), in_specs...  1.38 us
    ppermute x1, starting transfers between devices, body(): got = lax.ppermute(theirs, 'col', pairs)  1.38 us
    ppermute x1, waiting for transfers between devices, body(): lax.ppermute(second, 'col', pairs)  1.07 us
  transfers between devices with their start and end apart: 3, of which 1 were waited for; matrix products, arithmetic and copies ran while one was open for 0% of the time, Pallas kernels for 3%

profile of v4, /device:TPU:1, one launch (start us, length us, event | category | flops | bytes accessed | tf_op | source)
XLA Modules:
  0.0 45.3 jit_solution(17013920600573898041)
XLA Ops:
  0.0 3.2 %collective-permute-start = (f32[64,64]{1,0:T(8,128)}, f32[64,64]{1,0:T(8,128)S(1)}, u32[]{:S(2)}, u32[]{:S(2)}) collective-permute-start(f32[64,64]{1,0:T(8,128)} %param.4), channel_id=1, source_target_pairs={{0,1},{1,0},{2,3},{3,2},{4,5},{5,4},{6,7},{7,6},{8,9},{9,8},{10,11... | collective-permute-start | bytes 49160 | tf_op jit(solution)/shard_map/ppermute | solution.py:208
  3.2 1.1 %collective-permute-done.second_ref = f32[64,64]{1,0:T(8,128)S(1)} collective-permute-done((f32[64,64]{1,0:T(8,128)}, f32[64,64]{1,0:T(8,128)S(1)}, u32[]{:S(2)}, u32[]{:S(2)}) %collective-permute-start) | collective-permute-done | bytes 16416 | tf_op jit(solution)/shard_map/ppermute | solution.py:208
  4.3 0.3 collective-permute-start.1
  4.7 0.1 shard_map.37
  4.8 13.2 %all_to_all.10.rows_ref = f32[16,32,128]{2,1,0:T(8,128)S(1)} all-to-all(f32[16,32,128]{2,1,0:T(8,128)S(1)} %shard_map.37), channel_id=1, replica_groups=mesh['row'=16,'col'=16] {'row'}, dimensions={0} | all-to-all | bytes 524288 | tf_op jit(solution)/shard_map/all_to_all | solution.py:217
  17.9 0.0 collective-permute-done.1.tensor_ref
  17.9 2.4 %shard_map.38 = (f32[280,128]{1,0:T(8,128)S(1)}, bf16[2,1024,128]{2,1,0:T(8,128)(2,1)S(1)}) custom-call(f32[2,1024,1024]{2,1,0:T(8,128)S(1)} %collective-permute-done.1.tensor_ref, f32[16,32,128]{2,1,0:T(8,128)S(1)} %all_to_all.10.rows_ref, f32[2,64]{1,0:T(2,128)} %third_ref.1), custom_call_target="tpu_custom_call" | custom-call | bytes 4194304 | tf_op jit(solution)/shard_map/pallas_call | solution.py:218
  20.4 1.4 %collective-permute-start.2 = (f32[280,128]{1,0:T(8,128)S(1)}, f32[280,128]{1,0:T(8,128)S(1)}, u32[]{:S(2)}, u32[]{:S(2)}) collective-permute-start(f32[280,128]{1,0:T(8,128)S(1)} %get-tuple-element.12.theirs_ref), channel_id=1, source_target_pairs={{0,1},{1,0},{2,3},{3,2},{4,5},{5,4},{6,7},{7,6},{8,9},{9,8},{10,11... | collective-permute-start | bytes 430088 | tf_op jit(solution)/shard_map/ppermute | solution.py:230
  21.7 1.4 %shard_map.39.own_ref = f32[256,128]{1,0:T(8,128)S(1)} custom-call(f32[2,1024,1024]{2,1,0:T(8,128)S(1)} %collective-permute-done.1.tensor_ref, bf16[2,1024,128]{2,1,0:T(8,128)(2,1)S(1)} %get-tuple-element.11.weights), custom_call_target="tpu_custom_call" | custom-call | bytes 4194304 | tf_op jit(solution)/shard_map/pallas_call | solution.py:231
  23.1 0.0 collective-permute-done.2.got_ref
  23.2 19.6 %all_to_all.11.got_ref = f32[8,56,128]{2,1,0:T(8,128)S(1)} all-to-all(f32[8,56,128]{2,1,0:T(8,128)S(1)} %shard_map.40), channel_id=1, replica_groups={{0,2,4,6,8,10,12,14},{1,3,5,7,9,11,13,15},{16,18,20,22,24,26,28,30},{17..., dimensions={0} | all-to-all | bytes 458752 | tf_op jit(solution)/shard_map/all_to_all | solution.py:247
  42.8 2.5 %shard_map.41 = f32[64,64]{1,0:T(8,128)} custom-call(f32[8,56,128]{2,1,0:T(8,128)S(1)} %all_to_all.11.got_ref), custom_call_target="tpu_custom_call" | custom-call | tf_op jit(solution)/shard_map/pallas_call | solution.py:248
  (1 shorter events, 0.0 us)
Async XLA Ops:
  0.0 4.3 %collective-permute-start = (f32[64,64]{1,0:T(8,128)}, f32[64,64]{1,0:T(8,128)S(1)}, u32[]{:S(2)}, u32[]{:S(2)}) collective-permute-start(f32[64,64]{1,0:T(8,128)} %param.4), channel_id=1, source_target_pairs={{0,1},{1,0},{2,3},{3,2},{4,5},{5,4},{6,7},{7,6},{8,9},{9,8},{10,11... | collective-permute-start | bytes 49160 | tf_op jit(solution)/shard_map/ppermute | solution.py:208
  4.3 13.6 %collective-permute-start.1 = (f32[2,1024,1024]{2,1,0:T(8,128)}, f32[2,1024,1024]{2,1,0:T(8,128)S(1)}, u32[]{:S(2)}, u32[]{:S(2)}) collective-permute-start(f32[2,1024,1024]{2,1,0:T(8,128)} %param.3), channel_id=1, source_target_pairs={{0,1},{1,0},{2,3},{3,2},{4,5},{5,4},{6,7},{7,6},{8,9},{9,8},{10,11... | collective-permute-start | bytes 25165832 | tf_op jit(solution)/shard_map/ppermute | solution.py:209
  20.4 2.8 %collective-permute-start.2 = (f32[280,128]{1,0:T(8,128)S(1)}, f32[280,128]{1,0:T(8,128)S(1)}, u32[]{:S(2)}, u32[]{:S(2)}) collective-permute-start(f32[280,128]{1,0:T(8,128)S(1)} %get-tuple-element.12.theirs_ref), channel_id=1, source_target_pairs={{0,1},{1,0},{2,3},{3,2},{4,5},{5,4},{6,7},{7,6},{8,9},{9,8},{10,11... | collective-permute-start | bytes 430088 | tf_op jit(solution)/shard_map/ppermute | solution.py:230

commit v5 on v4

--- a/solution.py
+++ b/solution.py
@@ -13,6 +13,8 @@
 STRIP = 8
 GROUP = 4
 GRAM_ROWS = 24
+CHIPS = (5, 6, 7, 0, 1, 2, 3, 4)
+PLANE = (10, 11, 12, 13, 14, 15, 0, 1, 2, 3, 4, 5, 6, 7, 8, 9)
 
 
 def vmem():
@@ -35,7 +37,14 @@
     return jax.ShapeDtypeStruct(dims, dtype)
 
 
-def pack_kernel(second_ref, out_ref):
+def scale_kernel(third_ref, out_ref):
+    slices = third_ref.shape[0]
+    out_ref[:slices, :RANK] = third_ref[...]
+    out_ref[:slices, RANK:] = third_ref[...]
+
+
+def pack_kernel(second_ref, scale_ref, out_ref):
+    del scale_ref
     packed = jnp.concatenate([second_ref[:HALF, :], second_ref[HALF:, :]], axis=1)
     for peer in range(out_ref.shape[0]):
         out_ref[peer] = packed
@@ -49,14 +58,14 @@
     return lax.broadcasted_iota(jnp.int32, (rows, LANES), 1) < RANK
 
 
-def make_weights(rows_ref, scale, weights):
+def make_weights(rows_ref, scale_ref, weights):
     left = lower_lanes(HALF)
-    for peer in range(rows_ref.shape[0]):
-        here = rows_ref[peer]
+    for slot, peer in enumerate(PLANE):
+        here = rows_ref[slot]
         there = swap(here)
         for k in range(weights.shape[0]):
-            a = here * scale[k : k + 1, :]
-            b = there * scale[k : k + 1, :]
+            a = here * scale_ref[k : k + 1, :]
+            b = there * scale_ref[k : k + 1, :]
             a_hi = a.astype(BF16).astype(F32)
             b_hi = b.astype(BF16).astype(F32)
             first = jnp.where(left, a_hi, b - b_hi)
@@ -98,25 +107,21 @@
     return jnp.concatenate([top, jnp.concatenate(corner, axis=1)], axis=0)
 
 
-def partner_kernel(tensor_ref, rows_ref, third_ref, out_ref, weights, scale, sem):
+def partner_kernel(tensor_ref, rows_ref, scale_ref, out_ref, weights):
     core = lax.rem(lax.axis_index("col"), 2)
-    slices = weights.shape[0]
-    copy = pltpu.make_async_copy(third_ref, scale.at[:slices, :], sem)
-    copy.start()
+    make_weights(rows_ref, scale_ref, weights)
     flat = rows_ref[...].reshape(-1, LANES)
     both = lax.dot_general(
         flat, flat, (((0,), (0,)), ((), ())),
         precision=lax.Precision.HIGHEST, preferred_element_type=F32,
     )
-    copy.wait()
-    third = scale[:slices, :]
+    third = scale_ref[: weights.shape[0], :]
     outer = lax.dot_general(
         third, third, (((0,), (0,)), ((), ())),
         precision=lax.Precision.HIGHEST, preferred_element_type=F32,
     )
-    gram = (both[:RANK, :RANK] + both[RANK:, RANK:]) * outer
+    gram = (both[:RANK, :RANK] + both[RANK:, RANK:]) * outer[:RANK, :RANK]
     out_ref[2 * GROUP * HALF :, :] = pack_gram(gram)
-    make_weights(rows_ref, jnp.concatenate([third, third], axis=1), weights)
     for first in range(0, 2 * GROUP, GROUP):
         multiply(tensor_ref, weights, out_ref, first, 1 - core)
 
@@ -132,8 +137,9 @@
     gram = theirs_ref[chips * HALF :, :] + got_ref[chips * HALF :, :]
     for chip in range(chips):
         part = slice(chip * HALF, (chip + 1) * HALF)
-        out_ref[chip, :HALF, :] = own_ref[part, :] + got_ref[part, :]
-        out_ref[chip, HALF:, :] = gram
+        slot = CHIPS.index(chip)
+        out_ref[slot, :HALF, :] = own_ref[part, :] + got_ref[part, :]
+        out_ref[slot, HALF:, :] = gram
 
 
 def lane(x, c):
@@ -205,28 +211,36 @@
     chips = cols // 2
     slices, own, inner = tensor.shape
     pairs = [(i, i ^ 1) for i in range(cols)]
-    second, tensor = lax.optimization_barrier((lax.ppermute(second, "col", pairs), tensor))
+    second = lax.ppermute(second, "col", pairs)
+    scale = pl.pallas_call(
+        scale_kernel,
+        out_shape=shape(STRIP, LANES),
+        in_specs=[vmem()],
+        out_specs=vmem(),
+        compiler_params=limit(4),
+        cost_estimate=pl.CostEstimate(flops=0, bytes_accessed=4 << 20, transcendentals=0),
+    )(third)
+    second, scale, tensor = lax.optimization_barrier((second, scale, tensor))
     tensor = lax.ppermute(tensor, "col", pairs)
     copies = pl.pallas_call(
         pack_kernel,
         out_shape=shape(rows, HALF, LANES),
-        in_specs=[vmem()],
-        out_specs=vmem(),
-        compiler_params=limit(4),
-    )(second)
-    block = lax.all_to_all(copies, "row", 0, 0)
+        in_specs=[vmem(), vmem()],
+        out_specs=vmem(),
+        compiler_params=limit(4),
+    )(second, scale)
+    block = lax.all_to_all(copies, "row", 0, 0, axis_index_groups=[list(PLANE)])
     theirs, weights = pl.pallas_call(
         partner_kernel,
         out_shape=(
             shape(chips * HALF + GRAM_ROWS, LANES),
             shape(slices, inner, LANES, dtype=BF16),
         ),
-        in_specs=[vmem(), vmem(), anywhere()],
+        in_specs=[vmem(), vmem(), vmem()],
         out_specs=(vmem(), vmem()),
-        scratch_shapes=[pltpu.VMEM((STRIP, RANK), F32), pltpu.SemaphoreType.DMA],
         compiler_params=limit(12),
         cost_estimate=pl.CostEstimate(flops=0, bytes_accessed=4 << 20, transcendentals=0),
-    )(tensor, block, in_hbm(third))
+    )(tensor, block, scale)
     got = lax.ppermute(theirs, "col", pairs)
     mine = pl.pallas_call(
         own_kernel,
@@ -243,7 +257,7 @@
         out_specs=vmem(),
         compiler_params=limit(4),
     )(mine, theirs, got)
-    sides = [[2 * chip + core for chip in range(chips)] for core in range(2)]
+    sides = [[2 * chip + core for chip in CHIPS] for core in range(2)]
     total = lax.all_to_all(sent, "col", 0, 0, axis_index_groups=sides)
     return pl.pallas_call(
         solve_kernel,

time: 45.4 us -> 36.9 us (0.81)
  the two profiles are of different devices: /device:TPU:1 before, /device:TPU:10 now
where the time goes in v5:
time: 36.9 us; the launch traced here: 36.8 us
  blocking collectives  28.4 us (77%)
  Pallas kernels  5.84 us (16%)
  waiting for transfers between devices  1.39 us (4%)
  local copies, waits for them, and re-layouts  0.68 us (2%)
  starting transfers between devices  0.41 us (1%)
    all_to_all x1, blocking collectives, body(): total = lax.all_to_all(sent, 'col', 0, 0, axis_index_groups=sides)  16 us
    all_to_all x1, blocking collectives, body(): block = lax.all_to_all(copies, 'row', 0, 0, axis_index_groups=[list(PLANE)])  12.4 us
    pallas_call x1, Pallas kernels, body(): pl.pallas_call(solve_kernel, out_shape=shape(RANK, RANK), in_specs=[vmem(...  2.48 us
    pallas_call x1, Pallas kernels, body(): pl.pallas_call(partner_kernel, out_shape=(shape(chips * HALF + GRAM_ROWS,...  1.83 us
    pallas_call x1, Pallas kernels, body(): pl.pallas_call(own_kernel, out_shape=shape(chips * HALF, LANES), in_specs...  1.35 us
  transfers between devices with their start and end apart: 3, of which 2 were waited for; matrix products, arithmetic and copies ran while one was open for 0% of the time, Pallas kernels for 4%

profile of v5, /device:TPU:10, one launch (start us, length us, event | category | flops | bytes accessed | tf_op | source)
XLA Modules:
  0.0 36.8 jit_solution(6794029351856285195)
XLA Ops:
  0.0 0.0 collective-permute-start
  0.0 0.0 copy-start
  0.0 0.7 %copy-done = f32[2,64]{1,0:T(2,128)S(1)} copy-done((f32[2,64]{1,0:T(2,128)S(1)}, f32[2,64]{1,0:T(2,128)}, u32[]{:S(2)}) %copy-start) | copy-done | bytes 536
  0.7 0.1 shard_map.37.scale_ref
  0.8 0.7 %collective-permute-done.second_ref = f32[64,64]{1,0:T(8,128)S(1)} collective-permute-done((f32[64,64]{1,0:T(8,128)}, f32[64,64]{1,0:T(8,128)S(1)}, u32[]{:S(2)}, u32[]{:S(2)}) %collective-permute-start) | collective-permute-done | bytes 16416 | tf_op jit(solution)/shard_map/ppermute | solution.py:214
  1.4 0.2 collective-permute-start.1
  1.6 0.1 shard_map.38
  1.7 12.4 %all_to_all.10.rows_ref = f32[16,32,128]{2,1,0:T(8,128)S(1)} all-to-all(f32[16,32,128]{2,1,0:T(8,128)S(1)} %shard_map.38), channel_id=1, replica_groups={{160,176,192,208,224,240,0,16,32,48,64,80,96,112,128,144},{161,177,193,..., dimensions={0} | all-to-all | bytes 524288 | tf_op jit(solution)/shard_map/all_to_all | solution.py:232
  14.1 0.7 %collective-permute-done.1.tensor_ref = f32[2,1024,1024]{2,1,0:T(8,128)S(1)} collective-permute-done((f32[2,1024,1024]{2,1,0:T(8,128)}, f32[2,1024,1024]{2,1,0:T(8,128)S(1)}, u32[]{:S(2)}, u32[]{:S(2)}) %collective-permute-start.1) | collective-permute-done | bytes 8388640 | tf_op jit(solution)/shard_map/ppermute | solution.py:224
  14.8 1.8 %shard_map.39 = (f32[280,128]{1,0:T(8,128)S(1)}, bf16[2,1024,128]{2,1,0:T(8,128)(2,1)S(1)}) custom-call(f32[2,1024,1024]{2,1,0:T(8,128)S(1)} %collective-permute-done.1.tensor_ref, f32[16,32,128]{2,1,0:T(8,128)S(1)} %all_to_all.10.rows_ref, f32[8,128]{1,0:T(8,128)S(1)} %shard_map.37.scale_ref), custom_call_target="tpu_custom_call" | custom-call | bytes 4194304 | tf_op jit(solution)/shard_map/pallas_call | solution.py:233
  16.6 0.2 collective-permute-start.2
  16.9 1.4 %shard_map.40.own_ref = f32[256,128]{1,0:T(8,128)S(1)} custom-call(f32[2,1024,1024]{2,1,0:T(8,128)S(1)} %collective-permute-done.1.tensor_ref, bf16[2,1024,128]{2,1,0:T(8,128)(2,1)S(1)} %get-tuple-element.13.weights), custom_call_target="tpu_custom_call" | custom-call | bytes 4194304 | tf_op jit(solution)/shard_map/pallas_call | solution.py:245
  18.2 0.0 collective-permute-done.2.got_ref
  18.3 16.0 %all_to_all.11.got_ref = f32[8,56,128]{2,1,0:T(8,128)S(1)} all-to-all(f32[8,56,128]{2,1,0:T(8,128)S(1)} %shard_map.41), channel_id=1, replica_groups={{10,12,14,0,2,4,6,8},{11,13,15,1,3,5,7,9},{26,28,30,16,18,20,22,24},{27..., dimensions={0} | all-to-all | bytes 458752 | tf_op jit(solution)/shard_map/all_to_all | solution.py:261
  34.3 2.5 %shard_map.42 = f32[64,64]{1,0:T(8,128)} custom-call(f32[8,56,128]{2,1,0:T(8,128)S(1)} %all_to_all.11.got_ref), custom_call_target="tpu_custom_call" | custom-call | tf_op jit(solution)/shard_map/pallas_call | solution.py:262
  (1 shorter events, 0.0 us)
Async XLA Ops:
  0.0 1.4 %collective-permute-start = (f32[64,64]{1,0:T(8,128)}, f32[64,64]{1,0:T(8,128)S(1)}, u32[]{:S(2)}, u32[]{:S(2)}) collective-permute-start(f32[64,64]{1,0:T(8,128)} %param.4), channel_id=1, source_target_pairs={{0,1},{1,0},{2,3},{3,2},{4,5},{5,4},{6,7},{7,6},{8,9},{9,8},{10,11... | collective-permute-start | bytes 49160 | tf_op jit(solution)/shard_map/ppermute | solution.py:214
  0.0 0.7 %copy-start = (f32[2,64]{1,0:T(2,128)S(1)}, f32[2,64]{1,0:T(2,128)}, u32[]{:S(2)}) copy-start(f32[2,64]{1,0:T(2,128)} %third_ref.1) | copy-start | bytes 1540
  1.4 13.4 %collective-permute-start.1 = (f32[2,1024,1024]{2,1,0:T(8,128)}, f32[2,1024,1024]{2,1,0:T(8,128)S(1)}, u32[]{:S(2)}, u32[]{:S(2)}) collective-permute-start(f32[2,1024,1024]{2,1,0:T(8,128)} %param.3), channel_id=1, source_target_pairs={{0,1},{1,0},{2,3},{3,2},{4,5},{5,4},{6,7},{7,6},{8,9},{9,8},{10,11... | collective-permute-start | bytes 25165832 | tf_op jit(solution)/shard_map/ppermute | solution.py:224
  16.6 1.6 %collective-permute-start.2 = (f32[280,128]{1,0:T(8,128)S(1)}, f32[280,128]{1,0:T(8,128)S(1)}, u32[]{:S(2)}, u32[]{:S(2)}) collective-permute-start(f32[280,128]{1,0:T(8,128)S(1)} %get-tuple-element.14.theirs_ref), channel_id=1, source_target_pairs={{0,1},{1,0},{2,3},{3,2},{4,5},{5,4},{6,7},{7,6},{8,9},{9,8},{10,11... | collective-permute-start | bytes 430088 | tf_op jit(solution)/shard_map/ppermute | solution.py:244

commit v6 on v5

--- a/solution.py
+++ b/solution.py
@@ -13,7 +13,7 @@
 STRIP = 8
 GROUP = 4
 GRAM_ROWS = 24
-CHIPS = (5, 6, 7, 0, 1, 2, 3, 4)
+CHIPS = (5, 6, 4, 7, 0, 3, 1, 2)
 PLANE = (10, 11, 12, 13, 14, 15, 0, 1, 2, 3, 4, 5, 6, 7, 8, 9)
 
 
@@ -107,8 +107,7 @@
     return jnp.concatenate([top, jnp.concatenate(corner, axis=1)], axis=0)
 
 
-def partner_kernel(tensor_ref, rows_ref, scale_ref, out_ref, weights):
-    core = lax.rem(lax.axis_index("col"), 2)
+def weights_kernel(rows_ref, scale_ref, weights, gram_ref):
     make_weights(rows_ref, scale_ref, weights)
     flat = rows_ref[...].reshape(-1, LANES)
     both = lax.dot_general(
@@ -121,9 +120,14 @@
         precision=lax.Precision.HIGHEST, preferred_element_type=F32,
     )
     gram = (both[:RANK, :RANK] + both[RANK:, RANK:]) * outer[:RANK, :RANK]
-    out_ref[2 * GROUP * HALF :, :] = pack_gram(gram)
+    gram_ref[...] = pack_gram(gram)
+
+
+def partner_kernel(tensor_ref, weights, gram_ref, out_ref):
+    core = lax.rem(lax.axis_index("col"), 2)
     for first in range(0, 2 * GROUP, GROUP):
         multiply(tensor_ref, weights, out_ref, first, 1 - core)
+    out_ref[2 * GROUP * HALF :, :] = gram_ref[...]
 
 
 def own_kernel(tensor_ref, weights, out_ref):
@@ -230,17 +234,22 @@
         compiler_params=limit(4),
     )(second, scale)
     block = lax.all_to_all(copies, "row", 0, 0, axis_index_groups=[list(PLANE)])
-    theirs, weights = pl.pallas_call(
+    weights, gram = pl.pallas_call(
+        weights_kernel,
+        out_shape=(shape(slices, inner, LANES, dtype=BF16), shape(GRAM_ROWS, LANES)),
+        in_specs=[vmem(), vmem()],
+        out_specs=(vmem(), vmem()),
+        compiler_params=limit(8),
+        cost_estimate=pl.CostEstimate(flops=0, bytes_accessed=4 << 20, transcendentals=0),
+    )(block, scale)
+    theirs = pl.pallas_call(
         partner_kernel,
-        out_shape=(
-            shape(chips * HALF + GRAM_ROWS, LANES),
-            shape(slices, inner, LANES, dtype=BF16),
-        ),
+        out_shape=shape(chips * HALF + GRAM_ROWS, LANES),
         in_specs=[vmem(), vmem(), vmem()],
-        out_specs=(vmem(), vmem()),
+        out_specs=vmem(),
         compiler_params=limit(12),
         cost_estimate=pl.CostEstimate(flops=0, bytes_accessed=4 << 20, transcendentals=0),
-    )(tensor, block, scale)
+    )(tensor, weights, gram)
     got = lax.ppermute(theirs, "col", pairs)
     mine = pl.pallas_call(
         own_kernel,

time: 36.9 us -> 36.5 us (0.989)
  the two profiles are of different devices: /device:TPU:10 before, /device:TPU:1 now
where the time goes in v6:
time: 36.5 us; the launch traced here: 36.3 us
  blocking collectives  23.3 us (64%)
  Pallas kernels  6.05 us (17%)
  starting transfers between devices  4.01 us (11%)
  waiting for transfers between devices  2.18 us (6%)
  local copies, waits for them, and re-layouts  0.68 us (2%)
    all_to_all x1, blocking collectives, body(): total = lax.all_to_all(sent, 'col', 0, 0, axis_index_groups=sides)  12.9 us
    all_to_all x1, blocking collectives, body(): block = lax.all_to_all(copies, 'row', 0, 0, axis_index_groups=[list(PLANE)])  10.5 us
    ppermute x1, starting transfers between devices, body(): second = lax.ppermute(second, 'col', pairs)  3.24 us
    pallas_call x1, Pallas kernels, body(): pl.pallas_call(solve_kernel, out_shape=shape(RANK, RANK), in_specs=[vmem(...  2.48 us
    ppermute x1, waiting for transfers between devices, body(): tensor = lax.ppermute(tensor, 'col', pairs)  1.85 us
    pallas_call x1, Pallas kernels, body(): pl.pallas_call(partner_kernel, out_shape=shape(chips * HALF + GRAM_ROWS,...  1.4 us
    pallas_call x1, Pallas kernels, body(): pl.pallas_call(own_kernel, out_shape=shape(chips * HALF, LANES), in_specs...  1.39 us
  transfers between devices with their start and end apart: 3, of which 2 were waited for; matrix products, arithmetic and copies ran while one was open for 0% of the time, Pallas kernels for 6%

profile of v6, /device:TPU:1, one launch (start us, length us, event | category | flops | bytes accessed | tf_op | source)
XLA Modules:
  0.0 36.3 jit_solution(3608479194241349455)
XLA Ops:
  0.0 3.2 %collective-permute-start = (f32[64,64]{1,0:T(8,128)}, f32[64,64]{1,0:T(8,128)S(1)}, u32[]{:S(2)}, u32[]{:S(2)}) collective-permute-start(f32[64,64]{1,0:T(8,128)} %param.4), channel_id=1, source_target_pairs={{0,1},{1,0},{2,3},{3,2},{4,5},{5,4},{6,7},{7,6},{8,9},{9,8},{10,11... | collective-permute-start | bytes 49160 | tf_op jit(solution)/shard_map/ppermute | solution.py:218
  3.2 0.0 copy-start
  3.2 0.7 %copy-done = f32[2,64]{1,0:T(2,128)S(1)} copy-done((f32[2,64]{1,0:T(2,128)S(1)}, f32[2,64]{1,0:T(2,128)}, u32[]{:S(2)}) %copy-start) | copy-done | bytes 536
  3.9 0.1 shard_map.37.scale_ref
  4.0 0.3 collective-permute-done.second_ref
  4.3 0.3 collective-permute-start.1
  4.7 0.1 shard_map.38
  4.8 10.5 %all_to_all.10.rows_ref = f32[16,32,128]{2,1,0:T(8,128)S(1)} all-to-all(f32[16,32,128]{2,1,0:T(8,128)S(1)} %shard_map.38), channel_id=1, replica_groups={{160,176,192,208,224,240,0,16,32,48,64,80,96,112,128,144},{161,177,193,..., dimensions={0} | all-to-all | bytes 524288 | tf_op jit(solution)/shard_map/all_to_all | solution.py:236
  15.2 0.6 %shard_map.39 = (bf16[2,1024,128]{2,1,0:T(8,128)(2,1)S(1)}, f32[24,128]{1,0:T(8,128)S(1)}) custom-call(f32[16,32,128]{2,1,0:T(8,128)S(1)} %all_to_all.10.rows_ref, f32[8,128]{1,0:T(8,128)S(1)} %shard_map.37.scale_ref), custom_call_target="tpu_custom_call" | custom-call | bytes 4194304 | tf_op jit(solution)/shard_map/pallas_call | solution.py:237
  15.8 1.9 %collective-permute-done.1.tensor_ref = f32[2,1024,1024]{2,1,0:T(8,128)S(1)} collective-permute-done((f32[2,1024,1024]{2,1,0:T(8,128)}, f32[2,1024,1024]{2,1,0:T(8,128)S(1)}, u32[]{:S(2)}, u32[]{:S(2)}) %collective-permute-start.1) | collective-permute-done | bytes 8388640 | tf_op jit(solution)/shard_map/ppermute | solution.py:228
  17.7 1.4 %shard_map.41.theirs_ref = f32[280,128]{1,0:T(8,128)S(1)} custom-call(f32[2,1024,1024]{2,1,0:T(8,128)S(1)} %collective-permute-done.1.tensor_ref, bf16[2,1024,128]{2,1,0:T(8,128)(2,1)S(1)} %get-tuple-element.13.weights, f32[24,128]{1,0:T(8,128)S(1)} %get-tuple-element.14.gram_ref), custom_call_target="tpu_custom_call" | custom-call | bytes 4194304 | tf_op jit(solution)/shard_map/pallas_call | solution.py:245
  19.1 0.4 %collective-permute-start.2 = (f32[280,128]{1,0:T(8,128)S(1)}, f32[280,128]{1,0:T(8,128)S(1)}, u32[]{:S(2)}, u32[]{:S(2)}) collective-permute-start(f32[280,128]{1,0:T(8,128)S(1)} %shard_map.41.theirs_ref), channel_id=1, source_target_pairs={{0,1},{1,0},{2,3},{3,2},{4,5},{5,4},{6,7},{7,6},{8,9},{9,8},{10,11... | collective-permute-start | bytes 430088 | tf_op jit(solution)/shard_map/ppermute | solution.py:253
  19.5 1.4 %shard_map.40.own_ref = f32[256,128]{1,0:T(8,128)S(1)} custom-call(f32[2,1024,1024]{2,1,0:T(8,128)S(1)} %collective-permute-done.1.tensor_ref, bf16[2,1024,128]{2,1,0:T(8,128)(2,1)S(1)} %get-tuple-element.13.weights), custom_call_target="tpu_custom_call" | custom-call | bytes 4194304 | tf_op jit(solution)/shard_map/pallas_call | solution.py:254
  20.9 0.0 collective-permute-done.2.got_ref
  20.9 12.9 %all_to_all.11.got_ref = f32[8,56,128]{2,1,0:T(8,128)S(1)} all-to-all(f32[8,56,128]{2,1,0:T(8,128)S(1)} %shard_map.42), channel_id=1, replica_groups={{10,12,8,14,0,6,2,4},{11,13,9,15,1,7,3,5},{26,28,24,30,16,22,18,20},{27..., dimensions={0} | all-to-all | bytes 458752 | tf_op jit(solution)/shard_map/all_to_all | solution.py:270
  33.8 2.5 %shard_map.43 = f32[64,64]{1,0:T(8,128)} custom-call(f32[8,56,128]{2,1,0:T(8,128)S(1)} %all_to_all.11.got_ref), custom_call_target="tpu_custom_call" | custom-call | tf_op jit(solution)/shard_map/pallas_call | solution.py:271
  (1 shorter events, 0.0 us)
Async XLA Ops:
  0.0 4.3 %collective-permute-start = (f32[64,64]{1,0:T(8,128)}, f32[64,64]{1,0:T(8,128)S(1)}, u32[]{:S(2)}, u32[]{:S(2)}) collective-permute-start(f32[64,64]{1,0:T(8,128)} %param.4), channel_id=1, source_target_pairs={{0,1},{1,0},{2,3},{3,2},{4,5},{5,4},{6,7},{7,6},{8,9},{9,8},{10,11... | collective-permute-start | bytes 49160 | tf_op jit(solution)/shard_map/ppermute | solution.py:218
  3.2 0.7 %copy-start = (f32[2,64]{1,0:T(2,128)S(1)}, f32[2,64]{1,0:T(2,128)}, u32[]{:S(2)}) copy-start(f32[2,64]{1,0:T(2,128)} %third_ref.1) | copy-start | bytes 1540
  4.3 13.4 %collective-permute-start.1 = (f32[2,1024,1024]{2,1,0:T(8,128)}, f32[2,1024,1024]{2,1,0:T(8,128)S(1)}, u32[]{:S(2)}, u32[]{:S(2)}) collective-permute-start(f32[2,1024,1024]{2,1,0:T(8,128)} %param.3), channel_id=1, source_target_pairs={{0,1},{1,0},{2,3},{3,2},{4,5},{5,4},{6,7},{7,6},{8,9},{9,8},{10,11... | collective-permute-start | bytes 25165832 | tf_op jit(solution)/shard_map/ppermute | solution.py:228
  19.1 1.8 %collective-permute-start.2 = (f32[280,128]{1,0:T(8,128)S(1)}, f32[280,128]{1,0:T(8,128)S(1)}, u32[]{:S(2)}, u32[]{:S(2)}) collective-permute-start(f32[280,128]{1,0:T(8,128)S(1)} %shard_map.41.theirs_ref), channel_id=1, source_target_pairs={{0,1},{1,0},{2,3},{3,2},{4,5},{5,4},{6,7},{7,6},{8,9},{9,8},{10,11... | collective-permute-start | bytes 430088 | tf_op jit(solution)/shard_map/ppermute | solution.py:253

commit v7 on v6

--- a/solution.py
+++ b/solution.py
@@ -224,7 +224,6 @@
         compiler_params=limit(4),
         cost_estimate=pl.CostEstimate(flops=0, bytes_accessed=4 << 20, transcendentals=0),
     )(third)
-    second, scale, tensor = lax.optimization_barrier((second, scale, tensor))
     tensor = lax.ppermute(tensor, "col", pairs)
     copies = pl.pallas_call(
         pack_kernel,
@@ -232,6 +231,7 @@
         in_specs=[vmem(), vmem()],
         out_specs=vmem(),
         compiler_params=limit(4),
+        cost_estimate=pl.CostEstimate(flops=100000000000, bytes_accessed=0, transcendentals=0),
     )(second, scale)
     block = lax.all_to_all(copies, "row", 0, 0, axis_index_groups=[list(PLANE)])
     weights, gram = pl.pallas_call(

time: 36.5 us -> 36.1 us (0.989)
  blocking collectives: 23.3 us -> 24.1 us
  waiting for transfers between devices: 2.18 us -> 1.63 us
  starting transfers between devices: 4.01 us -> 3.47 us
    all_to_all x1, blocking collectives: 12.9 us -> 13.8 us  [body(): total = lax.all_to_all(sent, 'col', 0, 0, axis_index_groups=sides)]
    ppermute x1, waiting for transfers between devices: 1.85 us -> 1.31 us  [body(): tensor = lax.ppermute(tensor, 'col', pairs)]
where the time goes in v7:
time: 36.1 us; the launch traced here: 36 us
  blocking collectives  24.1 us (67%)
  Pallas kernels  6.05 us (17%)
  starting transfers between devices  3.47 us (10%)
  waiting for transfers between devices  1.63 us (5%)
  local copies, waits for them, and re-layouts  0.68 us (2%)
    all_to_all x1, blocking collectives, body(): total = lax.all_to_all(sent, 'col', 0, 0, axis_index_groups=sides)  13.8 us
    all_to_all x1, blocking collectives, body(): block = lax.all_to_all(copies, 'row', 0, 0, axis_index_groups=[list(PLANE)])  10.3 us
    ppermute x1, starting transfers between devices, body(): second = lax.ppermute(second, 'col', pairs)  3.24 us
    pallas_call x1, Pallas kernels, body(): pl.pallas_call(solve_kernel, out_shape=shape(RANK, RANK), in_specs=[vmem(...  2.48 us
    pallas_call x1, Pallas kernels, body(): pl.pallas_call(partner_kernel, out_shape=shape(chips * HALF + GRAM_ROWS,...  1.4 us
    pallas_call x1, Pallas kernels, body(): pl.pallas_call(own_kernel, out_shape=shape(chips * HALF, LANES), in_specs...  1.39 us
    ppermute x1, waiting for transfers between devices, body(): tensor = lax.ppermute(tensor, 'col', pairs)  1.31 us
  transfers between devices with their start and end apart: 3, of which 2 were waited for; matrix products, arithmetic and copies ran while one was open for 0% of the time, Pallas kernels for 6%

profile of v7, /device:TPU:1, one launch (start us, length us, event | category | flops | bytes accessed | tf_op | source)
XLA Modules:
  0.0 36.0 jit_solution(16317467295522102397)
XLA Ops:
  0.0 3.2 %collective-permute-start.1 = (f32[64,64]{1,0:T(8,128)}, f32[64,64]{1,0:T(8,128)S(1)}, u32[]{:S(2)}, u32[]{:S(2)}) collective-permute-start(f32[64,64]{1,0:T(8,128)} %param.4), channel_id=1, source_target_pairs={{0,1},{1,0},{2,3},{3,2},{4,5},{5,4},{6,7},{7,6},{8,9},{9,8},{10,11... | collective-permute-start | bytes 49160 | tf_op jit(solution)/shard_map/ppermute | solution.py:218
  3.2 0.0 collective-permute-start
  3.2 0.0 copy-start
  3.2 0.7 %copy-done = f32[2,64]{1,0:T(2,128)S(1)} copy-done((f32[2,64]{1,0:T(2,128)S(1)}, f32[2,64]{1,0:T(2,128)}, u32[]{:S(2)}) %copy-start) | copy-done | bytes 536
  3.9 0.1 shard_map.37.scale_ref
  4.0 0.3 collective-permute-done.1.second_ref
  4.3 0.1 shard_map.38
  4.4 10.3 %all_to_all.10.rows_ref = f32[16,32,128]{2,1,0:T(8,128)S(1)} all-to-all(f32[16,32,128]{2,1,0:T(8,128)S(1)} %shard_map.38), channel_id=1, replica_groups={{160,176,192,208,224,240,0,16,32,48,64,80,96,112,128,144},{161,177,193,..., dimensions={0} | all-to-all | bytes 524288 | tf_op jit(solution)/shard_map/all_to_all | solution.py:236
  14.7 0.6 %shard_map.39 = (bf16[2,1024,128]{2,1,0:T(8,128)(2,1)S(1)}, f32[24,128]{1,0:T(8,128)S(1)}) custom-call(f32[16,32,128]{2,1,0:T(8,128)S(1)} %all_to_all.10.rows_ref, f32[8,128]{1,0:T(8,128)S(1)} %shard_map.37.scale_ref), custom_call_target="tpu_custom_call" | custom-call | bytes 4194304 | tf_op jit(solution)/shard_map/pallas_call | solution.py:237
  15.3 1.3 %collective-permute-done.tensor_ref = f32[2,1024,1024]{2,1,0:T(8,128)S(1)} collective-permute-done((f32[2,1024,1024]{2,1,0:T(8,128)}, f32[2,1024,1024]{2,1,0:T(8,128)S(1)}, u32[]{:S(2)}, u32[]{:S(2)}) %collective-permute-start) | collective-permute-done | bytes 8388640 | tf_op jit(solution)/shard_map/ppermute | solution.py:227
  16.6 1.4 %shard_map.41.theirs_ref = f32[280,128]{1,0:T(8,128)S(1)} custom-call(f32[2,1024,1024]{2,1,0:T(8,128)S(1)} %collective-permute-done.tensor_ref, bf16[2,1024,128]{2,1,0:T(8,128)(2,1)S(1)} %get-tuple-element.7.weights, f32[24,128]{1,0:T(8,128)S(1)} %get-tuple-element.8.gram_ref), custom_call_target="tpu_custom_call" | custom-call | bytes 4194304 | tf_op jit(solution)/shard_map/pallas_call | solution.py:245
  18.0 0.2 collective-permute-start.2
  18.2 1.4 %shard_map.40.own_ref = f32[256,128]{1,0:T(8,128)S(1)} custom-call(f32[2,1024,1024]{2,1,0:T(8,128)S(1)} %collective-permute-done.tensor_ref, bf16[2,1024,128]{2,1,0:T(8,128)(2,1)S(1)} %get-tuple-element.7.weights), custom_call_target="tpu_custom_call" | custom-call | bytes 4194304 | tf_op jit(solution)/shard_map/pallas_call | solution.py:254
  19.6 0.0 collective-permute-done.2.got_ref
  19.7 13.8 %all_to_all.11.got_ref = f32[8,56,128]{2,1,0:T(8,128)S(1)} all-to-all(f32[8,56,128]{2,1,0:T(8,128)S(1)} %shard_map.42), channel_id=1, replica_groups={{10,12,8,14,0,6,2,4},{11,13,9,15,1,7,3,5},{26,28,24,30,16,22,18,20},{27..., dimensions={0} | all-to-all | bytes 458752 | tf_op jit(solution)/shard_map/all_to_all | solution.py:270
  33.5 2.5 %shard_map.43 = f32[64,64]{1,0:T(8,128)} custom-call(f32[8,56,128]{2,1,0:T(8,128)S(1)} %all_to_all.11.got_ref), custom_call_target="tpu_custom_call" | custom-call | tf_op jit(solution)/shard_map/pallas_call | solution.py:271
  (1 shorter events, 0.0 us)
Async XLA Ops:
  0.0 4.3 %collective-permute-start.1 = (f32[64,64]{1,0:T(8,128)}, f32[64,64]{1,0:T(8,128)S(1)}, u32[]{:S(2)}, u32[]{:S(2)}) collective-permute-start(f32[64,64]{1,0:T(8,128)} %param.4), channel_id=1, source_target_pairs={{0,1},{1,0},{2,3},{3,2},{4,5},{5,4},{6,7},{7,6},{8,9},{9,8},{10,11... | collective-permute-start | bytes 49160 | tf_op jit(solution)/shard_map/ppermute | solution.py:218
  3.2 13.4 %collective-permute-start = (f32[2,1024,1024]{2,1,0:T(8,128)}, f32[2,1024,1024]{2,1,0:T(8,128)S(1)}, u32[]{:S(2)}, u32[]{:S(2)}) collective-permute-start(f32[2,1024,1024]{2,1,0:T(8,128)} %param.3), channel_id=1, source_target_pairs={{0,1},{1,0},{2,3},{3,2},{4,5},{5,4},{6,7},{7,6},{8,9},{9,8},{10,11... | collective-permute-start | bytes 25165832 | tf_op jit(solution)/shard_map/ppermute | solution.py:227
  3.2 0.7 %copy-start = (f32[2,64]{1,0:T(2,128)S(1)}, f32[2,64]{1,0:T(2,128)}, u32[]{:S(2)}) copy-start(f32[2,64]{1,0:T(2,128)} %third_ref.1) | copy-start | bytes 1540
  18.0 1.6 %collective-permute-start.2 = (f32[280,128]{1,0:T(8,128)S(1)}, f32[280,128]{1,0:T(8,128)S(1)}, u32[]{:S(2)}, u32[]{:S(2)}) collective-permute-start(f32[280,128]{1,0:T(8,128)S(1)} %shard_map.41.theirs_ref), channel_id=1, source_target_pairs={{0,1},{1,0},{2,3},{3,2},{4,5},{5,4},{6,7},{7,6},{8,9},{9,8},{10,11... | collective-permute-start | bytes 430088 | tf_op jit(solution)/shard_map/ppermute | solution.py:253

commit v8 on v7

--- a/solution.py
+++ b/solution.py
@@ -11,7 +11,7 @@
 LANES = 128
 HALF = 32
 STRIP = 8
-GROUP = 4
+GROUP = 8
 GRAM_ROWS = 24
 CHIPS = (5, 6, 4, 7, 0, 3, 1, 2)
 PLANE = (10, 11, 12, 13, 14, 15, 0, 1, 2, 3, 4, 5, 6, 7, 8, 9)
@@ -107,32 +107,43 @@
     return jnp.concatenate([top, jnp.concatenate(corner, axis=1)], axis=0)
 
 
+def inner_products(a, b):
+    return lax.dot_general(a, b, (((0,), (0,)), ((), ())), preferred_element_type=F32)
+
+
+def own_quarters(x):
+    return x[:RANK, :RANK] + x[RANK:, RANK:]
+
+
 def weights_kernel(rows_ref, scale_ref, weights, gram_ref):
     make_weights(rows_ref, scale_ref, weights)
     flat = rows_ref[...].reshape(-1, LANES)
-    both = lax.dot_general(
-        flat, flat, (((0,), (0,)), ((), ())),
-        precision=lax.Precision.HIGHEST, preferred_element_type=F32,
-    )
+    high = flat.astype(BF16)
+    rest = flat - high.astype(F32)
+    middle = rest.astype(BF16)
+    low = (rest - middle.astype(F32)).astype(BF16)
+    cross = inner_products(high, jnp.concatenate([middle, low], axis=1))
+    cross = own_quarters(cross[:, :LANES] + cross[:, LANES:])
+    square = own_quarters(inner_products(high, high) + inner_products(middle, middle))
     third = scale_ref[: weights.shape[0], :]
     outer = lax.dot_general(
         third, third, (((0,), (0,)), ((), ())),
         precision=lax.Precision.HIGHEST, preferred_element_type=F32,
     )
-    gram = (both[:RANK, :RANK] + both[RANK:, RANK:]) * outer[:RANK, :RANK]
+    gram = (square + cross + cross.T) * outer[:RANK, :RANK]
     gram_ref[...] = pack_gram(gram)
 
 
 def partner_kernel(tensor_ref, weights, gram_ref, out_ref):
     core = lax.rem(lax.axis_index("col"), 2)
-    for first in range(0, 2 * GROUP, GROUP):
+    for first in range(0, len(CHIPS), GROUP):
         multiply(tensor_ref, weights, out_ref, first, 1 - core)
-    out_ref[2 * GROUP * HALF :, :] = gram_ref[...]
+    out_ref[len(CHIPS) * HALF :, :] = gram_ref[...]
 
 
 def own_kernel(tensor_ref, weights, out_ref):
     core = lax.rem(lax.axis_index("col"), 2)
-    for first in range(0, 2 * GROUP, GROUP):
+    for first in range(0, len(CHIPS), GROUP):
         multiply(tensor_ref, weights, out_ref, first, core)
 
 

time: 36.1 us -> 36 us (level)
  no operation moved by 1% of the time
where the time goes in v8:
time: 36 us; the launch traced here: 35.7 us
  blocking collectives  24 us (67%)
  Pallas kernels  5.86 us (16%)
  starting transfers between devices  3.47 us (10%)
  waiting for transfers between devices  1.73 us (5%)
  local copies, waits for them, and re-layouts  0.68 us (2%)
    all_to_all x1, blocking collectives, body(): total = lax.all_to_all(sent, 'col', 0, 0, axis_index_groups=sides)  13.7 us
    all_to_all x1, blocking collectives, body(): block = lax.all_to_all(copies, 'row', 0, 0, axis_index_groups=[list(PLANE)])  10.3 us
    ppermute x1, starting transfers between devices, body(): second = lax.ppermute(second, 'col', pairs)  3.24 us
    pallas_call x1, Pallas kernels, body(): pl.pallas_call(solve_kernel, out_shape=shape(RANK, RANK), in_specs=[vmem(...  2.48 us
    ppermute x1, waiting for transfers between devices, body(): tensor = lax.ppermute(tensor, 'col', pairs)  1.41 us
    pallas_call x1, Pallas kernels, body(): pl.pallas_call(partner_kernel, out_shape=shape(chips * HALF + GRAM_ROWS,...  1.35 us
    pallas_call x1, Pallas kernels, body(): pl.pallas_call(own_kernel, out_shape=shape(chips * HALF, LANES), in_specs...  1.35 us
  transfers between devices with their start and end apart: 3, of which 2 were waited for; matrix products, arithmetic and copies ran while one was open for 0% of the time, Pallas kernels for 6%

profile of v8, /device:TPU:1, one launch (start us, length us, event | category | flops | bytes accessed | tf_op | source)
XLA Modules:
  0.0 35.7 jit_solution(17182243232666349141)
XLA Ops:
  0.0 3.2 %collective-permute-start.1 = (f32[64,64]{1,0:T(8,128)}, f32[64,64]{1,0:T(8,128)S(1)}, u32[]{:S(2)}, u32[]{:S(2)}) collective-permute-start(f32[64,64]{1,0:T(8,128)} %param.4), channel_id=1, source_target_pairs={{0,1},{1,0},{2,3},{3,2},{4,5},{5,4},{6,7},{7,6},{8,9},{9,8},{10,11... | collective-permute-start | bytes 49160 | tf_op jit(solution)/shard_map/ppermute | solution.py:229
  3.2 0.0 collective-permute-start
  3.2 0.0 copy-start
  3.2 0.7 %copy-done = f32[2,64]{1,0:T(2,128)S(1)} copy-done((f32[2,64]{1,0:T(2,128)S(1)}, f32[2,64]{1,0:T(2,128)}, u32[]{:S(2)}) %copy-start) | copy-done | bytes 536
  3.9 0.1 shard_map.37.scale_ref
  4.0 0.3 collective-permute-done.1.second_ref
  4.3 0.1 shard_map.38
  4.4 10.3 %all_to_all.10.rows_ref = f32[16,32,128]{2,1,0:T(8,128)S(1)} all-to-all(f32[16,32,128]{2,1,0:T(8,128)S(1)} %shard_map.38), channel_id=1, replica_groups={{160,176,192,208,224,240,0,16,32,48,64,80,96,112,128,144},{161,177,193,..., dimensions={0} | all-to-all | bytes 524288 | tf_op jit(solution)/shard_map/all_to_all | solution.py:247
  14.7 0.5 %shard_map.39 = (bf16[2,1024,128]{2,1,0:T(8,128)(2,1)S(1)}, f32[24,128]{1,0:T(8,128)S(1)}) custom-call(f32[16,32,128]{2,1,0:T(8,128)S(1)} %all_to_all.10.rows_ref, f32[8,128]{1,0:T(8,128)S(1)} %shard_map.37.scale_ref), custom_call_target="tpu_custom_call" | custom-call | bytes 4194304 | tf_op jit(solution)/shard_map/pallas_call | solution.py:248
  15.2 1.4 %collective-permute-done.tensor_ref = f32[2,1024,1024]{2,1,0:T(8,128)S(1)} collective-permute-done((f32[2,1024,1024]{2,1,0:T(8,128)}, f32[2,1024,1024]{2,1,0:T(8,128)S(1)}, u32[]{:S(2)}, u32[]{:S(2)}) %collective-permute-start) | collective-permute-done | bytes 8388640 | tf_op jit(solution)/shard_map/ppermute | solution.py:238
  16.6 1.4 %shard_map.41.theirs_ref = f32[280,128]{1,0:T(8,128)S(1)} custom-call(f32[2,1024,1024]{2,1,0:T(8,128)S(1)} %collective-permute-done.tensor_ref, bf16[2,1024,128]{2,1,0:T(8,128)(2,1)S(1)} %get-tuple-element.7.weights, f32[24,128]{1,0:T(8,128)S(1)} %get-tuple-element.8.gram_ref), custom_call_target="tpu_custom_call" | custom-call | bytes 4194304 | tf_op jit(solution)/shard_map/pallas_call | solution.py:256
  18.0 0.2 collective-permute-start.2
  18.2 1.3 %shard_map.40.own_ref = f32[256,128]{1,0:T(8,128)S(1)} custom-call(f32[2,1024,1024]{2,1,0:T(8,128)S(1)} %collective-permute-done.tensor_ref, bf16[2,1024,128]{2,1,0:T(8,128)(2,1)S(1)} %get-tuple-element.7.weights), custom_call_target="tpu_custom_call" | custom-call | bytes 4194304 | tf_op jit(solution)/shard_map/pallas_call | solution.py:265
  19.6 0.0 collective-permute-done.2.got_ref
  19.6 13.7 %all_to_all.11.got_ref = f32[8,56,128]{2,1,0:T(8,128)S(1)} all-to-all(f32[8,56,128]{2,1,0:T(8,128)S(1)} %shard_map.42), channel_id=1, replica_groups={{10,12,8,14,0,6,2,4},{11,13,9,15,1,7,3,5},{26,28,24,30,16,22,18,20},{27..., dimensions={0} | all-to-all | bytes 458752 | tf_op jit(solution)/shard_map/all_to_all | solution.py:281
  33.3 2.5 %shard_map.43 = f32[64,64]{1,0:T(8,128)} custom-call(f32[8,56,128]{2,1,0:T(8,128)S(1)} %all_to_all.11.got_ref), custom_call_target="tpu_custom_call" | custom-call | tf_op jit(solution)/shard_map/pallas_call | solution.py:282
  (1 shorter events, 0.0 us)
Async XLA Ops:
  0.0 4.3 %collective-permute-start.1 = (f32[64,64]{1,0:T(8,128)}, f32[64,64]{1,0:T(8,128)S(1)}, u32[]{:S(2)}, u32[]{:S(2)}) collective-permute-start(f32[64,64]{1,0:T(8,128)} %param.4), channel_id=1, source_target_pairs={{0,1},{1,0},{2,3},{3,2},{4,5},{5,4},{6,7},{7,6},{8,9},{9,8},{10,11... | collective-permute-start | bytes 49160 | tf_op jit(solution)/shard_map/ppermute | solution.py:229
  3.2 13.4 %collective-permute-start = (f32[2,1024,1024]{2,1,0:T(8,128)}, f32[2,1024,1024]{2,1,0:T(8,128)S(1)}, u32[]{:S(2)}, u32[]{:S(2)}) collective-permute-start(f32[2,1024,1024]{2,1,0:T(8,128)} %param.3), channel_id=1, source_target_pairs={{0,1},{1,0},{2,3},{3,2},{4,5},{5,4},{6,7},{7,6},{8,9},{9,8},{10,11... | collective-permute-start | bytes 25165832 | tf_op jit(solution)/shard_map/ppermute | solution.py:238
  3.2 0.7 %copy-start = (f32[2,64]{1,0:T(2,128)S(1)}, f32[2,64]{1,0:T(2,128)}, u32[]{:S(2)}) copy-start(f32[2,64]{1,0:T(2,128)} %third_ref.1) | copy-start | bytes 1540
  18.0 1.6 %collective-permute-start.2 = (f32[280,128]{1,0:T(8,128)S(1)}, f32[280,128]{1,0:T(8,128)S(1)}, u32[]{:S(2)}, u32[]{:S(2)}) collective-permute-start(f32[280,128]{1,0:T(8,128)S(1)} %shard_map.41.theirs_ref), channel_id=1, source_target_pairs={{0,1},{1,0},{2,3},{3,2},{4,5},{5,4},{6,7},{7,6},{8,9},{9,8},{10,11... | collective-permute-start | bytes 430088 | tf_op jit(solution)/shard_map/ppermute | solution.py:264

commit v9 on v8

--- a/solution.py
+++ b/solution.py
@@ -157,6 +157,10 @@
         out_ref[slot, HALF:, :] = gram
 
 
+def row(x, r):
+    return jnp.broadcast_to(x[r : r + 1, :], (STRIP, LANES))
+
+
 def lane(x, c):
     return jnp.broadcast_to(x[:, c : c + 1], (STRIP, LANES))
 
@@ -169,8 +173,12 @@
 
 def eliminate(diag, others, row_id):
     diag = list(diag)
+    pivot = row(diag[0], 0)
     for j in range(STRIP):
-        inv = 1.0 / jnp.broadcast_to(diag[j][j : j + 1, :], (STRIP, LANES))
+        inv = 1.0 / pivot
+        if j + 1 < STRIP:
+            corner = row(diag[j], j + 1) * row(diag[j + 1], j)
+            pivot = row(diag[j + 1], j + 1) - corner * inv
         ratio = jnp.where(row_id == j, 1.0 - inv, diag[j] * inv)
         for m in range(j + 1, STRIP):
             diag[m] = diag[m] - ratio * diag[m][j : j + 1, :]
@@ -211,11 +219,10 @@
                 - pairwise([cols[p + 1][k] * ahead[m][k : k + 1, :] for k in range(STRIP)])
                 for m in range(STRIP)
             ]
+        spread = [row(pivot, m) for m in range(STRIP)]
         for q in range(strips):
             if q != p:
-                a[q] = a[q] - pairwise(
-                    [cols[q][m] * pivot[m : m + 1, :] for m in range(STRIP)]
-                )
+                a[q] = a[q] - pairwise([cols[q][m] * spread[m] for m in range(STRIP)])
     solved = jnp.concatenate(a, axis=0)
     out_ref[...] = jnp.transpose(jnp.concatenate([solved, solved], axis=0))[RANK:, :RANK]
 

time: 36 us -> 35.9 us (level)
  no operation moved by 1% of the time
where the time goes in v9:
time: 35.9 us; the launch traced here: 35.7 us
  blocking collectives  24 us (67%)
  Pallas kernels  5.82 us (16%)
  starting transfers between devices  3.47 us (10%)
  waiting for transfers between devices  1.73 us (5%)
  local copies, waits for them, and re-layouts  0.68 us (2%)
    all_to_all x1, blocking collectives, body(): total = lax.all_to_all(sent, 'col', 0, 0, axis_index_groups=sides)  13.7 us
    all_to_all x1, blocking collectives, body(): block = lax.all_to_all(copies, 'row', 0, 0, axis_index_groups=[list(PLANE)])  10.3 us
    ppermute x1, starting transfers between devices, body(): second = lax.ppermute(second, 'col', pairs)  3.24 us
    pallas_call x1, Pallas kernels, body(): pl.pallas_call(solve_kernel, out_shape=shape(RANK, RANK), in_specs=[vmem(...  2.44 us
    ppermute x1, waiting for transfers between devices, body(): tensor = lax.ppermute(tensor, 'col', pairs)  1.41 us
    pallas_call x1, Pallas kernels, body(): pl.pallas_call(partner_kernel, out_shape=shape(chips * HALF + GRAM_ROWS,...  1.35 us
    pallas_call x1, Pallas kernels, body(): pl.pallas_call(own_kernel, out_shape=shape(chips * HALF, LANES), in_specs...  1.35 us
  transfers between devices with their start and end apart: 3, of which 2 were waited for; matrix products, arithmetic and copies ran while one was open for 0% of the time, Pallas kernels for 6%

profile of v9, /device:TPU:1, one launch (start us, length us, event | category | flops | bytes accessed | tf_op | source)
XLA Modules:
  0.0 35.7 jit_solution(915552891816930494)
XLA Ops:
  0.0 3.2 %collective-permute-start.1 = (f32[64,64]{1,0:T(8,128)}, f32[64,64]{1,0:T(8,128)S(1)}, u32[]{:S(2)}, u32[]{:S(2)}) collective-permute-start(f32[64,64]{1,0:T(8,128)} %param.4), channel_id=1, source_target_pairs={{0,1},{1,0},{2,3},{3,2},{4,5},{5,4},{6,7},{7,6},{8,9},{9,8},{10,11... | collective-permute-start | bytes 49160 | tf_op jit(solution)/shard_map/ppermute | solution.py:236
  3.2 0.0 collective-permute-start
  3.2 0.0 copy-start
  3.2 0.7 %copy-done = f32[2,64]{1,0:T(2,128)S(1)} copy-done((f32[2,64]{1,0:T(2,128)S(1)}, f32[2,64]{1,0:T(2,128)}, u32[]{:S(2)}) %copy-start) | copy-done | bytes 536
  3.9 0.1 shard_map.37.scale_ref
  4.0 0.3 collective-permute-done.1.second_ref
  4.3 0.1 shard_map.38
  4.4 10.3 %all_to_all.10.rows_ref = f32[16,32,128]{2,1,0:T(8,128)S(1)} all-to-all(f32[16,32,128]{2,1,0:T(8,128)S(1)} %shard_map.38), channel_id=1, replica_groups={{160,176,192,208,224,240,0,16,32,48,64,80,96,112,128,144},{161,177,193,..., dimensions={0} | all-to-all | bytes 524288 | tf_op jit(solution)/shard_map/all_to_all | solution.py:254
  14.7 0.5 %shard_map.39 = (bf16[2,1024,128]{2,1,0:T(8,128)(2,1)S(1)}, f32[24,128]{1,0:T(8,128)S(1)}) custom-call(f32[16,32,128]{2,1,0:T(8,128)S(1)} %all_to_all.10.rows_ref, f32[8,128]{1,0:T(8,128)S(1)} %shard_map.37.scale_ref), custom_call_target="tpu_custom_call" | custom-call | bytes 4194304 | tf_op jit(solution)/shard_map/pallas_call | solution.py:255
  15.2 1.4 %collective-permute-done.tensor_ref = f32[2,1024,1024]{2,1,0:T(8,128)S(1)} collective-permute-done((f32[2,1024,1024]{2,1,0:T(8,128)}, f32[2,1024,1024]{2,1,0:T(8,128)S(1)}, u32[]{:S(2)}, u32[]{:S(2)}) %collective-permute-start) | collective-permute-done | bytes 8388640 | tf_op jit(solution)/shard_map/ppermute | solution.py:245
  16.6 1.4 %shard_map.41.theirs_ref = f32[280,128]{1,0:T(8,128)S(1)} custom-call(f32[2,1024,1024]{2,1,0:T(8,128)S(1)} %collective-permute-done.tensor_ref, bf16[2,1024,128]{2,1,0:T(8,128)(2,1)S(1)} %get-tuple-element.7.weights, f32[24,128]{1,0:T(8,128)S(1)} %get-tuple-element.8.gram_ref), custom_call_target="tpu_custom_call" | custom-call | bytes 4194304 | tf_op jit(solution)/shard_map/pallas_call | solution.py:263
  18.0 0.2 collective-permute-start.2
  18.2 1.3 %shard_map.40.own_ref = f32[256,128]{1,0:T(8,128)S(1)} custom-call(f32[2,1024,1024]{2,1,0:T(8,128)S(1)} %collective-permute-done.tensor_ref, bf16[2,1024,128]{2,1,0:T(8,128)(2,1)S(1)} %get-tuple-element.7.weights), custom_call_target="tpu_custom_call" | custom-call | bytes 4194304 | tf_op jit(solution)/shard_map/pallas_call | solution.py:272
  19.6 0.0 collective-permute-done.2.got_ref
  19.6 13.7 %all_to_all.11.got_ref = f32[8,56,128]{2,1,0:T(8,128)S(1)} all-to-all(f32[8,56,128]{2,1,0:T(8,128)S(1)} %shard_map.42), channel_id=1, replica_groups={{10,12,8,14,0,6,2,4},{11,13,9,15,1,7,3,5},{26,28,24,30,16,22,18,20},{27..., dimensions={0} | all-to-all | bytes 458752 | tf_op jit(solution)/shard_map/all_to_all | solution.py:288
  33.3 2.4 %shard_map.43 = f32[64,64]{1,0:T(8,128)} custom-call(f32[8,56,128]{2,1,0:T(8,128)S(1)} %all_to_all.11.got_ref), custom_call_target="tpu_custom_call" | custom-call | tf_op jit(solution)/shard_map/pallas_call | solution.py:289
  (1 shorter events, 0.0 us)
Async XLA Ops:
  0.0 4.3 %collective-permute-start.1 = (f32[64,64]{1,0:T(8,128)}, f32[64,64]{1,0:T(8,128)S(1)}, u32[]{:S(2)}, u32[]{:S(2)}) collective-permute-start(f32[64,64]{1,0:T(8,128)} %param.4), channel_id=1, source_target_pairs={{0,1},{1,0},{2,3},{3,2},{4,5},{5,4},{6,7},{7,6},{8,9},{9,8},{10,11... | collective-permute-start | bytes 49160 | tf_op jit(solution)/shard_map/ppermute | solution.py:236
  3.2 13.4 %collective-permute-start = (f32[2,1024,1024]{2,1,0:T(8,128)}, f32[2,1024,1024]{2,1,0:T(8,128)S(1)}, u32[]{:S(2)}, u32[]{:S(2)}) collective-permute-start(f32[2,1024,1024]{2,1,0:T(8,128)} %param.3), channel_id=1, source_target_pairs={{0,1},{1,0},{2,3},{3,2},{4,5},{5,4},{6,7},{7,6},{8,9},{9,8},{10,11... | collective-permute-start | bytes 25165832 | tf_op jit(solution)/shard_map/ppermute | solution.py:245
  3.2 0.7 %copy-start = (f32[2,64]{1,0:T(2,128)S(1)}, f32[2,64]{1,0:T(2,128)}, u32[]{:S(2)}) copy-start(f32[2,64]{1,0:T(2,128)} %third_ref.1) | copy-start | bytes 1540
  18.0 1.6 %collective-permute-start.2 = (f32[280,128]{1,0:T(8,128)S(1)}, f32[280,128]{1,0:T(8,128)S(1)}, u32[]{:S(2)}, u32[]{:S(2)}) collective-permute-start(f32[280,128]{1,0:T(8,128)S(1)} %shard_map.41.theirs_ref), channel_id=1, source_target_pairs={{0,1},{1,0},{2,3},{3,2},{4,5},{5,4},{6,7},{7,6},{8,9},{9,8},{10,11... | collective-permute-start | bytes 430088 | tf_op jit(solution)/shard_map/ppermute | solution.py:271

commit v10 on v8

--- a/solution.py
+++ b/solution.py
@@ -13,7 +13,7 @@
 STRIP = 8
 GROUP = 8
 GRAM_ROWS = 24
-CHIPS = (5, 6, 4, 7, 0, 3, 1, 2)
+CHIPS = (5, 4, 6, 7, 0, 3, 1, 2)
 PLANE = (10, 11, 12, 13, 14, 15, 0, 1, 2, 3, 4, 5, 6, 7, 8, 9)
 
 

time: 36 us -> 36.1 us (level)
  the two profiles are of different devices: /device:TPU:1 before, /device:TPU:4 now
where the time goes in v10:
time: 36.1 us; the launch traced here: 35.9 us
  blocking collectives  28.5 us (79%)
  Pallas kernels  5.88 us (16%)
  local copies, waits for them, and re-layouts  0.68 us (2%)
  starting transfers between devices  0.6 us (2%)
    all_to_all x1, blocking collectives, body(): total = lax.all_to_all(sent, 'col', 0, 0, axis_index_groups=sides)  15.8 us
    all_to_all x1, blocking collectives, body(): block = lax.all_to_all(copies, 'row', 0, 0, axis_index_groups=[list(PLANE)])  12.7 us
    pallas_call x1, Pallas kernels, body(): pl.pallas_call(solve_kernel, out_shape=shape(RANK, RANK), in_specs=[vmem(...  2.48 us
    pallas_call x1, Pallas kernels, body(): pl.pallas_call(partner_kernel, out_shape=shape(chips * HALF + GRAM_ROWS,...  1.36 us
    pallas_call x1, Pallas kernels, body(): pl.pallas_call(own_kernel, out_shape=shape(chips * HALF, LANES), in_specs...  1.35 us
  transfers between devices with their start and end apart: 3, of which 1 were waited for; matrix products, arithmetic and copies ran while one was open for 0% of the time, Pallas kernels for 6%

profile of v10, /device:TPU:4, one launch (start us, length us, event | category | flops | bytes accessed | tf_op | source)
XLA Modules:
  0.0 35.9 jit_solution(16430126452085523857)
XLA Ops:
  0.0 0.0 collective-permute-start.1
  0.0 0.5 %collective-permute-start = (f32[2,1024,1024]{2,1,0:T(8,128)}, f32[2,1024,1024]{2,1,0:T(8,128)S(1)}, u32[]{:S(2)}, u32[]{:S(2)}) collective-permute-start(f32[2,1024,1024]{2,1,0:T(8,128)} %param.3), channel_id=1, source_target_pairs={{0,1},{1,0},{2,3},{3,2},{4,5},{5,4},{6,7},{7,6},{8,9},{9,8},{10,11... | collective-permute-start | bytes 25165832 | tf_op jit(solution)/shard_map/ppermute | solution.py:238
  0.5 0.0 copy-start
  0.5 0.7 %copy-done = f32[2,64]{1,0:T(2,128)S(1)} copy-done((f32[2,64]{1,0:T(2,128)S(1)}, f32[2,64]{1,0:T(2,128)}, u32[]{:S(2)}) %copy-start) | copy-done | bytes 536
  1.2 0.1 shard_map.37.scale_ref
  1.3 0.2 collective-permute-done.1.second_ref
  1.4 0.1 shard_map.38
  1.5 12.7 %all_to_all.10.rows_ref = f32[16,32,128]{2,1,0:T(8,128)S(1)} all-to-all(f32[16,32,128]{2,1,0:T(8,128)S(1)} %shard_map.38), channel_id=1, replica_groups={{160,176,192,208,224,240,0,16,32,48,64,80,96,112,128,144},{161,177,193,..., dimensions={0} | all-to-all | bytes 524288 | tf_op jit(solution)/shard_map/all_to_all | solution.py:247
  14.2 0.5 %shard_map.39 = (bf16[2,1024,128]{2,1,0:T(8,128)(2,1)S(1)}, f32[24,128]{1,0:T(8,128)S(1)}) custom-call(f32[16,32,128]{2,1,0:T(8,128)S(1)} %all_to_all.10.rows_ref, f32[8,128]{1,0:T(8,128)S(1)} %shard_map.37.scale_ref), custom_call_target="tpu_custom_call" | custom-call | bytes 4194304 | tf_op jit(solution)/shard_map/pallas_call | solution.py:248
  14.7 0.0 collective-permute-done.tensor_ref
  14.7 1.4 %shard_map.41.theirs_ref = f32[280,128]{1,0:T(8,128)S(1)} custom-call(f32[2,1024,1024]{2,1,0:T(8,128)S(1)} %collective-permute-done.tensor_ref, bf16[2,1024,128]{2,1,0:T(8,128)(2,1)S(1)} %get-tuple-element.7.weights, f32[24,128]{1,0:T(8,128)S(1)} %get-tuple-element.8.gram_ref), custom_call_target="tpu_custom_call" | custom-call | bytes 4194304 | tf_op jit(solution)/shard_map/pallas_call | solution.py:256
  16.1 0.1 collective-permute-start.2
  16.2 1.4 %shard_map.40.own_ref = f32[256,128]{1,0:T(8,128)S(1)} custom-call(f32[2,1024,1024]{2,1,0:T(8,128)S(1)} %collective-permute-done.tensor_ref, bf16[2,1024,128]{2,1,0:T(8,128)(2,1)S(1)} %get-tuple-element.7.weights), custom_call_target="tpu_custom_call" | custom-call | bytes 4194304 | tf_op jit(solution)/shard_map/pallas_call | solution.py:265
  17.6 0.0 collective-permute-done.2.got_ref
  17.6 15.8 %all_to_all.11.got_ref = f32[8,56,128]{2,1,0:T(8,128)S(1)} all-to-all(f32[8,56,128]{2,1,0:T(8,128)S(1)} %shard_map.42), channel_id=1, replica_groups={{10,8,12,14,0,6,2,4},{11,9,13,15,1,7,3,5},{26,24,28,30,16,22,18,20},{27..., dimensions={0} | all-to-all | bytes 458752 | tf_op jit(solution)/shard_map/all_to_all | solution.py:281
  33.4 2.5 %shard_map.43 = f32[64,64]{1,0:T(8,128)} custom-call(f32[8,56,128]{2,1,0:T(8,128)S(1)} %all_to_all.11.got_ref), custom_call_target="tpu_custom_call" | custom-call | tf_op jit(solution)/shard_map/pallas_call | solution.py:282
  (1 shorter events, 0.0 us)
Async XLA Ops:
  0.0 1.4 %collective-permute-start.1 = (f32[64,64]{1,0:T(8,128)}, f32[64,64]{1,0:T(8,128)S(1)}, u32[]{:S(2)}, u32[]{:S(2)}) collective-permute-start(f32[64,64]{1,0:T(8,128)} %param.4), channel_id=1, source_target_pairs={{0,1},{1,0},{2,3},{3,2},{4,5},{5,4},{6,7},{7,6},{8,9},{9,8},{10,11... | collective-permute-start | bytes 49160 | tf_op jit(solution)/shard_map/ppermute | solution.py:229
  0.0 14.7 %collective-permute-start = (f32[2,1024,1024]{2,1,0:T(8,128)}, f32[2,1024,1024]{2,1,0:T(8,128)S(1)}, u32[]{:S(2)}, u32[]{:S(2)}) collective-permute-start(f32[2,1024,1024]{2,1,0:T(8,128)} %param.3), channel_id=1, source_target_pairs={{0,1},{1,0},{2,3},{3,2},{4,5},{5,4},{6,7},{7,6},{8,9},{9,8},{10,11... | collective-permute-start | bytes 25165832 | tf_op jit(solution)/shard_map/ppermute | solution.py:238
  0.5 0.7 %copy-start = (f32[2,64]{1,0:T(2,128)S(1)}, f32[2,64]{1,0:T(2,128)}, u32[]{:S(2)}) copy-start(f32[2,64]{1,0:T(2,128)} %third_ref.1) | copy-start | bytes 1540
  16.1 1.5 %collective-permute-start.2 = (f32[280,128]{1,0:T(8,128)S(1)}, f32[280,128]{1,0:T(8,128)S(1)}, u32[]{:S(2)}, u32[]{:S(2)}) collective-permute-start(f32[280,128]{1,0:T(8,128)S(1)} %shard_map.41.theirs_ref), channel_id=1, source_target_pairs={{0,1},{1,0},{2,3},{3,2},{4,5},{5,4},{6,7},{7,6},{8,9},{9,8},{10,11... | collective-permute-start | bytes 430088 | tf_op jit(solution)/shard_map/ppermute | solution.py:264
